TPU v7x, 32 devices: a whole 2x2x4 slice. The times are simulated.
32 devices in a mesh: section: 2 (over x), shard: 2 (over core), dp: 8 (over z, y).
Axes of the slice: x: 2, y: 2, z: 4, core: 2. Of those that a mesh axis runs over, the one named last changes fastest.
Arguments:
- inputs: bfloat16 [2, 2, 1024, 768], P(None, 'shard', 'dp'), may hold values from -6 to 6
- out_grad: bfloat16 [2, 2, 1024, 768], P(None, 'shard', 'dp'), may hold values from -6 to 6
- doc_lengths: int32 [2, 2, 4], P(None, 'shard'), may hold values from 1 to 897, 1024 in all within a row
- norm_gain: bfloat16 [2, 768], P('section', 'shard'), may hold values from 0.5 to 1.5
- w_z: bfloat16 [2, 768, 1536], P('section', 'shard'), may hold values from -0.21875 to 0.21875
- w_xbc: bfloat16 [2, 768, 1792], P('section', 'shard'), may hold values from -0.21875 to 0.21875
- w_dt: bfloat16 [2, 768, 24], P('section', 'shard'), may hold values from -0.21875 to 0.21875
- conv_w: bfloat16 [2, 4, 1792], P('section', None, 'shard'), may hold values from -3 to 3
- conv_b: bfloat16 [2, 1792], P('section', 'shard'), may hold values from -0.5 to 0.5
- dt_bias: bfloat16 [2, 24], P('section', 'shard'), may hold values from -2 to 0.5
- decay_rate: bfloat16 [2, 24], P('section', 'shard'), may hold values from 0.0009765625 to 0.125
- d_skip: bfloat16 [2, 24], P('section', 'shard'), may hold values from 0.5 to 1.5
- gate_gain: bfloat16 [2, 1536], P('section', 'shard'), may hold values from 0.5 to 1.5
- w_out: bfloat16 [2, 1536, 768], P('section', 'shard'), may hold values from -0.15625 to 0.15625
Outputs:
- activations: bfloat16 [2, 2, 2, 1024, 768], P('section', None, 'shard', 'dp')
- input_grads: bfloat16 [2, 2, 2, 1024, 768], P('section', None, 'shard', 'dp')
- grad_norm_gain: float32 [2, 768], P('section', 'shard')
- grad_w_z: float32 [2, 768, 1536], P('section', 'shard')
- grad_w_xbc: float32 [2, 768, 1792], P('section', 'shard')
- grad_w_dt: float32 [2, 768, 24], P('section', 'shard')
- grad_conv_w: float32 [2, 4, 1792], P('section', None, 'shard')
- grad_conv_b: float32 [2, 1792], P('section', 'shard')
- grad_dt_bias: float32 [2, 24], P('section', 'shard')
- grad_decay_rate: float32 [2, 24], P('section', 'shard')
- grad_d_skip: float32 [2, 24], P('section', 'shard')
- grad_gate_gain: float32 [2, 1536], P('section', 'shard')
- grad_w_out: float32 [2, 1536, 768], P('section', 'shard')
Inputs may be any that keep to these rules, and one draw needn't show every extreme that they name: `doc_lengths`: each row of 4 lengths sums to 1024, and its largest length is exactly 897.
All inputs are finite; a program needn't handle non-finite values.
Results may differ from a plain program's by a relative error of at most 0.02.
Values may be sent and summed in bfloat16 or wider, within the bound.
A program may use at most 192 MiB of HBM per device.

v0:
```python
import jax
import jax.numpy as jnp
from jax import lax
from jax.sharding import PartitionSpec as P

DI = 1536
H = 24
P_SIZE = 64
N = 128
KW = 4
XC = 1792


epsilon = 1e-05
highest = lax.Precision.HIGHEST


def passed_along(value, axis, steps):
    count = lax.axis_size(axis)
    first, last = (max(0, -steps), min(count, count - steps))
    return lax.ppermute(value, axis, [(source, source + steps) for source in range(first, last)])


def entering(array, axis, combine, identity):
    size, here = (lax.axis_size(axis), lax.axis_index(axis))
    everything = jax.tree.map(lambda part: lax.all_gather(part, axis), array)
    start = jax.tree.map(
        lambda part, zero: jnp.broadcast_to(jnp.asarray(zero, part.dtype), part.shape),
        array,
        identity,
    )

    def turn(k, before):
        reached = k < here
        new = combine(before, jax.tree.map(lambda part: part[k], everything))
        return jax.tree.map(lambda a, b: jnp.where(reached, a, b), new, before)

    return lax.fori_loop(0, size, turn, start)


def carried_in(array, axis, join, neutral):
    count = lax.axis_size(axis)
    place = lax.axis_index(axis)
    ahead = count - 1 - place
    gathered = jax.tree.map(
        lambda a, kind: lax.all_gather(a.astype(kind), axis),
        array,
        jax.tree.map(lambda a: jnp.bfloat16 if a.dtype == jnp.float32 else a.dtype, array),
    )
    state = jax.tree.map(lambda a, e: jnp.zeros_like(a) + jnp.asarray(e, a.dtype), array, neutral)

    def one(turn, state):
        source = count - 1 - turn
        return join(
            state,
            jax.tree.map(
                lambda a, own: lax.dynamic_index_in_dim(a, source, 0, False).astype(own.dtype),
                gathered,
                array,
            ),
        )

    return lax.fori_loop(0, ahead, one, state)


def rms_scale(values):
    return values * lax.rsqrt(jnp.mean(values * values, axis=-1, keepdims=True) + epsilon)


def norm_in(hidden, gain):
    return rms_scale(hidden) * gain[None, :]


def segment_ids(lengths, positions):
    ends = jnp.cumsum(lengths)
    return jnp.sum((positions[:, None] >= ends[None, :]).astype(jnp.int32), axis=1)


def col_product(left, right):
    return lax.dot_general(
        left, right, (((0,), (0,)), ((), ())), preferred_element_type=jnp.float32
    )


def row_product(left, right):
    return lax.dot_general(
        left, right, (((1,), (1,)), ((), ())), preferred_element_type=jnp.float32
    )


def chain_join(earlier, later):
    return (earlier[0] * later[0], later[0][:, None, None] * earlier[1] + later[1])


def conv_gate(extended, dt_raw, conv_w, conv_b, dt_bias, decay_rate, seg_ext):
    tok_rows = dt_raw.shape[0]
    own_seg = seg_ext[KW - 1 :]
    conv_sum = jnp.broadcast_to(conv_b[None, :], (tok_rows, conv_b.shape[0]))
    for tap_no in range(KW):
        same_doc = (seg_ext[tap_no : tap_no + tok_rows] == own_seg)[:, None].astype(jnp.float32)
        conv_sum = (
            conv_sum + conv_w[tap_no][None, :] * extended[tap_no : tap_no + tok_rows] * same_doc
        )
    activated = jax.nn.silu(conv_sum)
    dt_vals = jax.nn.softplus(dt_raw + dt_bias[None, :])
    cumul = jnp.cumsum(-dt_vals * decay_rate[None, :], axis=0)
    return (activated, dt_vals, cumul)


def split_low(activated):
    rounded = activated.astype(jnp.bfloat16).astype(jnp.float32)
    return (rounded[:, :DI], rounded[:, DI : DI + N], rounded[:, DI + N :])


def block_state(xs_vals, b_vals, dt_vals, cumul, own_seg, prior_seg):
    tok_rows = xs_vals.shape[0]
    scaled = xs_vals.reshape(tok_rows, H, P_SIZE) * dt_vals[:, :, None]
    last_seg = own_seg[-1]
    tail_decay = jnp.exp(cumul[-1][None, :] - cumul) * (own_seg == last_seg)[:, None].astype(
        jnp.float32
    )
    fresh_state = jnp.einsum(
        "jhp,jn->hpn", scaled * tail_decay[:, :, None], b_vals, precision=highest
    )
    through = jnp.exp(cumul[-1]) * (last_seg == prior_seg).astype(jnp.float32)
    return (through, fresh_state)


def mix_out(
    xs_vals, b_vals, c_vals, dt_vals, cumul, gate_z, state_in, d_skip, gate_gain, own_seg, prior_seg
):
    tok_rows = xs_vals.shape[0]
    heads_x = xs_vals.reshape(tok_rows, H, P_SIZE)
    index_row = jnp.arange(tok_rows, dtype=jnp.int32)
    keep_mask = (
        (index_row[:, None] >= index_row[None, :]) & (own_seg[:, None] == own_seg[None, :])
    )[None]
    cumul_t = cumul.T
    log_gaps = cumul_t[:, :, None] - cumul_t[:, None, :]
    weight = jnp.where(keep_mask, jnp.exp(jnp.where(keep_mask, log_gaps, 0.0)), 0.0)
    inner_cb = jnp.dot(c_vals, b_vals.T, precision=highest)
    scaled = heads_x * dt_vals[:, :, None]
    y_inner = jnp.einsum("hij,jhp->ihp", weight * inner_cb[None], scaled, precision=highest)
    entry_decay = jnp.exp(cumul) * (own_seg == prior_seg)[:, None].astype(jnp.float32)
    y_state = (
        jnp.einsum("in,hpn->ihp", c_vals, state_in, precision=highest) * entry_decay[:, :, None]
    )
    y_full = (y_inner + y_state + d_skip[None, :, None] * heads_x).reshape(tok_rows, DI)
    gated = y_full * jax.nn.silu(gate_z)
    return rms_scale(gated) * gate_gain[None, :]


def small_params(weights):
    return tuple((weights[index_no].astype(jnp.float32) for index_no in (0, 4, 5, 6, 7, 8, 9)))


def start_state():
    return (jnp.ones((H,), jnp.float32), jnp.zeros((H, P_SIZE, N), jnp.float32))


def layer_forward(hidden, weights, seg_ext):
    gain_in, conv_wf, conv_bf, bias_f, rate_f, skip_f, ggain_f = small_params(weights)
    tok_rows = hidden.shape[0]
    own_seg = seg_ext[KW - 1 :]
    prior_seg = seg_ext[KW - 2]
    normed_low = norm_in(hidden, gain_in).astype(jnp.bfloat16)
    gate_z = jnp.dot(normed_low, weights[1], preferred_element_type=jnp.float32)
    conv_raw = jnp.dot(normed_low, weights[2], preferred_element_type=jnp.float32).astype(
        jnp.bfloat16
    )
    dt_raw = jnp.dot(normed_low, weights[3], preferred_element_type=jnp.float32)
    rim_rows = passed_along(conv_raw[tok_rows - (KW - 1) :], "dp", 1)
    extended = jnp.concatenate([rim_rows, conv_raw], axis=0).astype(jnp.float32)
    activated, dt_vals, cumul = conv_gate(
        extended, dt_raw, conv_wf, conv_bf, bias_f, rate_f, seg_ext
    )
    xs_vals, b_vals, c_vals = split_low(activated)
    through, fresh_state = block_state(xs_vals, b_vals, dt_vals, cumul, own_seg, prior_seg)
    prefix = entering((through, fresh_state), "dp", chain_join, start_state())
    state_in = prefix[1]
    normed = mix_out(
        xs_vals,
        b_vals,
        c_vals,
        dt_vals,
        cumul,
        gate_z,
        state_in,
        skip_f,
        ggain_f,
        own_seg,
        prior_seg,
    )
    out_low = normed.astype(jnp.bfloat16)
    result = hidden + jnp.dot(out_low, weights[10], preferred_element_type=jnp.float32)
    return (result, (hidden, normed_low, gate_z, extended, dt_raw, state_in, out_low, seg_ext))


def weight_grads(pieces):
    left_norm, three_low, left_out, grad_low = pieces
    wide = col_product(left_norm, three_low)
    return (
        wide[:, :DI],
        wide[:, DI : DI + XC],
        wide[:, DI + XC :],
        col_product(left_out, grad_low),
    )


def layer_back(grad_out, kept, weights, valid):
    hidden, normed_low, gate_z, extended, dt_raw, state_in, out_low, seg_ext = kept
    gain_in, conv_wf, conv_bf, bias_f, rate_f, skip_f, ggain_f = small_params(weights)
    tok_rows = hidden.shape[0]
    own_seg = seg_ext[KW - 1 :]
    prior_seg = seg_ext[KW - 2]
    grad_low = grad_out.astype(jnp.bfloat16)
    grad_normed = row_product(grad_low, weights[10])

    def conv_fn(ext_arg, raw_arg, cw_arg, cb_arg, bias_arg, rate_arg):
        return conv_gate(ext_arg, raw_arg, cw_arg, cb_arg, bias_arg, rate_arg, seg_ext)

    (activated, dt_vals, cumul), conv_back = jax.vjp(
        conv_fn, extended, dt_raw, conv_wf, conv_bf, bias_f, rate_f
    )
    xs_vals, b_vals, c_vals = split_low(activated)

    def mix_fn(xs_arg, b_arg, c_arg, dt_arg, cum_arg, gate_arg, state_arg, skip_arg, ggain_arg):
        return mix_out(
            xs_arg,
            b_arg,
            c_arg,
            dt_arg,
            cum_arg,
            gate_arg,
            state_arg,
            skip_arg,
            ggain_arg,
            own_seg,
            prior_seg,
        )

    normed_unused, mix_back = jax.vjp(
        mix_fn, xs_vals, b_vals, c_vals, dt_vals, cumul, gate_z, state_in, skip_f, ggain_f
    )
    grad_xs, grad_b, grad_c, grad_dt, grad_cum, grad_gate, grad_state, grad_skip, grad_ggain = (
        mix_back(grad_normed)
    )

    def state_fn(xs_arg, b_arg, dt_arg, cum_arg):
        return block_state(xs_arg, b_arg, dt_arg, cum_arg, own_seg, prior_seg)

    (through, fresh_unused), state_back = jax.vjp(state_fn, xs_vals, b_vals, dt_vals, cumul)
    suffix = carried_in((through, grad_state), "dp", chain_join, start_state())
    later_grad = suffix[1]
    grad_through = jnp.sum(later_grad * state_in, axis=(1, 2))
    more_xs, more_b, more_dt, more_cum = state_back((grad_through, later_grad))
    grad_act = jnp.concatenate([grad_xs + more_xs, grad_b + more_b, grad_c], axis=1)
    grad_ext, grad_raw, grad_cw, grad_cb, grad_bias, grad_rate = conv_back(
        (grad_act, grad_dt + more_dt, grad_cum + more_cum)
    )
    from_next = passed_along(grad_ext[: KW - 1], "dp", -1)
    padding = jnp.zeros((tok_rows - (KW - 1), grad_ext.shape[1]), jnp.float32)
    grad_conv_in = grad_ext[KW - 1 :] + jnp.concatenate([padding, from_next], axis=0)
    gate_low = grad_gate.astype(jnp.bfloat16)
    conv_low = grad_conv_in.astype(jnp.bfloat16)
    step_low = grad_raw.astype(jnp.bfloat16)
    grad_normed_in = (
        row_product(gate_low, weights[1])
        + row_product(conv_low, weights[2])
        + row_product(step_low, weights[3])
    )
    value_unused, norm_back = jax.vjp(norm_in, hidden, gain_in)
    grad_hidden, grad_gain = norm_back(grad_normed_in)
    valid_low = valid.astype(jnp.bfloat16)
    three_low = jnp.concatenate([gate_low, conv_low, step_low], axis=1)
    pieces = (normed_low * valid_low, three_low, out_low * valid_low, grad_low)
    smalls = tuple(
        (
            member * valid
            for member in (grad_gain, grad_cw, grad_cb, grad_bias, grad_rate, grad_skip, grad_ggain)
        )
    )
    return (grad_hidden + grad_out, smalls, pieces)


def full_grads(smalls, larges):
    return (
        smalls[0],
        larges[0],
        larges[1],
        larges[2],
        smalls[1],
        smalls[2],
        smalls[3],
        smalls[4],
        smalls[5],
        smalls[6],
        larges[3],
    )


def per_device(
    inputs,
    out_grad,
    doc_lengths,
    norm_gain,
    w_z,
    w_xbc,
    w_dt,
    conv_w,
    conv_b,
    dt_bias,
    decay_rate,
    d_skip,
    gate_gain,
    w_out,
):
    section_no = lax.axis_index("section")
    is_first = section_no == 0
    micro = inputs.shape[0]
    tok_rows = inputs.shape[2]
    begin = lax.axis_index("dp") * tok_rows
    ext_pos = begin - (KW - 1) + jnp.arange(tok_rows + KW - 1, dtype=jnp.int32)
    gathered = (
        lax.all_gather(norm_gain, "shard", axis=1, tiled=True),
        lax.all_gather(w_z, "shard", axis=1, tiled=True),
        lax.all_gather(w_xbc, "shard", axis=1, tiled=True),
        lax.all_gather(w_dt, "shard", axis=1, tiled=True),
        lax.all_gather(conv_w, "shard", axis=2, tiled=True),
        lax.all_gather(conv_b, "shard", axis=1, tiled=True),
        lax.all_gather(dt_bias, "shard", axis=1, tiled=True),
        lax.all_gather(decay_rate, "shard", axis=1, tiled=True),
        lax.all_gather(d_skip, "shard", axis=1, tiled=True),
        lax.all_gather(gate_gain, "shard", axis=1, tiled=True),
        lax.all_gather(w_out, "shard", axis=1, tiled=True),
    )
    weights = tuple((member[0] for member in gathered))

    def pick(first_val, other_val):
        return jnp.where(is_first, first_val, other_val)

    received = jnp.zeros((tok_rows, inputs.shape[3]), jnp.bfloat16)
    kept_steps = []
    sent_steps = []
    for step_no in range(micro + 1):
        own_rows = inputs[min(step_no, micro - 1), 0]
        hidden = pick(own_rows, received).astype(jnp.float32)
        lengths = pick(doc_lengths[min(step_no, micro - 1), 0], doc_lengths[max(step_no - 1, 0), 0])
        seg_ext = segment_ids(lengths, ext_pos)
        result, kept = layer_forward(hidden, weights, seg_ext)
        sent = result.astype(jnp.bfloat16)
        if step_no < micro:
            received = passed_along(sent, "section", 1)
        kept_steps.append(kept)
        sent_steps.append(sent)
    back_rows = jnp.zeros((tok_rows, inputs.shape[3]), jnp.bfloat16)
    grad_steps = []
    piece_steps = []
    small_total = None
    totals = None
    for step_no in range(micro + 1):
        kept = jax.tree.map(
            pick, kept_steps[max(step_no - 1, 0)], kept_steps[min(step_no + 1, micro)]
        )
        grad_out = pick(back_rows, out_grad[min(step_no, micro - 1), 0]).astype(jnp.float32)
        valid = jnp.where(is_first, step_no >= 1, step_no < micro).astype(jnp.float32)
        grad_hidden, smalls, pieces = layer_back(grad_out, kept, weights, valid)
        grad_low = grad_hidden.astype(jnp.bfloat16)
        if step_no < micro:
            back_rows = passed_along(grad_low, "section", -1)
        grad_steps.append(grad_low)
        piece_steps.append(pieces)
        small_total = (
            smalls
            if small_total is None
            else tuple((left + right for left, right in zip(small_total, smalls)))
        )
    joined = tuple(
        (
            jnp.concatenate([piece[index_no] for piece in piece_steps], axis=0)
            for index_no in range(4)
        )
    )
    grads = full_grads(small_total, weight_grads(joined))
    lifted = tuple((member[None] for member in grads))
    totals = (
        lax.psum_scatter(
            lifted[0].astype(jnp.bfloat16), "shard", scatter_dimension=1, tiled=True
        ).astype(jnp.float32),
        lax.psum_scatter(
            lifted[1].astype(jnp.bfloat16), "shard", scatter_dimension=1, tiled=True
        ).astype(jnp.float32),
        lax.psum_scatter(
            lifted[2].astype(jnp.bfloat16), "shard", scatter_dimension=1, tiled=True
        ).astype(jnp.float32),
        lax.psum_scatter(
            lifted[3].astype(jnp.bfloat16), "shard", scatter_dimension=1, tiled=True
        ).astype(jnp.float32),
        lax.psum_scatter(
            lifted[4].astype(jnp.bfloat16), "shard", scatter_dimension=2, tiled=True
        ).astype(jnp.float32),
        lax.psum_scatter(
            lifted[5].astype(jnp.bfloat16), "shard", scatter_dimension=1, tiled=True
        ).astype(jnp.float32),
        lax.psum_scatter(
            lifted[6].astype(jnp.bfloat16), "shard", scatter_dimension=1, tiled=True
        ).astype(jnp.float32),
        lax.psum_scatter(
            lifted[7].astype(jnp.bfloat16), "shard", scatter_dimension=1, tiled=True
        ).astype(jnp.float32),
        lax.psum_scatter(
            lifted[8].astype(jnp.bfloat16), "shard", scatter_dimension=1, tiled=True
        ).astype(jnp.float32),
        lax.psum_scatter(
            lifted[9].astype(jnp.bfloat16), "shard", scatter_dimension=1, tiled=True
        ).astype(jnp.float32),
        lax.psum_scatter(
            lifted[10].astype(jnp.bfloat16), "shard", scatter_dimension=1, tiled=True
        ).astype(jnp.float32),
    )
    totals = (
        lax.psum(totals[0].astype(jnp.bfloat16), "dp").astype(jnp.float32),
        lax.psum(totals[1].astype(jnp.bfloat16), "dp").astype(jnp.float32),
        lax.psum(totals[2].astype(jnp.bfloat16), "dp").astype(jnp.float32),
        lax.psum(totals[3].astype(jnp.bfloat16), "dp").astype(jnp.float32),
        lax.psum(totals[4].astype(jnp.bfloat16), "dp").astype(jnp.float32),
        lax.psum(totals[5].astype(jnp.bfloat16), "dp").astype(jnp.float32),
        lax.psum(totals[6].astype(jnp.bfloat16), "dp").astype(jnp.float32),
        lax.psum(totals[7].astype(jnp.bfloat16), "dp").astype(jnp.float32),
        lax.psum(totals[8].astype(jnp.bfloat16), "dp").astype(jnp.float32),
        lax.psum(totals[9].astype(jnp.bfloat16), "dp").astype(jnp.float32),
        lax.psum(totals[10].astype(jnp.bfloat16), "dp").astype(jnp.float32),
    )
    activations = jnp.stack(
        [pick(sent_steps[micro_no], sent_steps[micro_no + 1]) for micro_no in range(micro)]
    )
    input_grads = jnp.stack(
        [pick(grad_steps[micro_no + 1], grad_steps[micro_no]) for micro_no in range(micro)]
    )
    activations = activations[None, :, None]
    input_grads = input_grads[None, :, None]
    return (
        activations,
        input_grads,
        totals[0],
        totals[1],
        totals[2],
        totals[3],
        totals[4],
        totals[5],
        totals[6],
        totals[7],
        totals[8],
        totals[9],
        totals[10],
    )


def solution(mesh):
    in_specs = (
        P(None, "shard", "dp", None),
        P(None, "shard", "dp", None),
        P(None, "shard", None),
        P("section", "shard"),
        P("section", "shard", None),
        P("section", "shard", None),
        P("section", "shard", None),
        P("section", None, "shard"),
        P("section", "shard"),
        P("section", "shard"),
        P("section", "shard"),
        P("section", "shard"),
        P("section", "shard"),
        P("section", "shard", None),
    )
    out_specs = (
        P("section", None, "shard", "dp", None),
        P("section", None, "shard", "dp", None),
        P("section", "shard"),
        P("section", "shard", None),
        P("section", "shard", None),
        P("section", "shard", None),
        P("section", None, "shard"),
        P("section", "shard"),
        P("section", "shard"),
        P("section", "shard"),
        P("section", "shard"),
        P("section", "shard"),
        P("section", "shard", None),
    )
    return jax.shard_map(
        per_device, mesh=mesh, in_specs=in_specs, out_specs=out_specs, check_vma=False
    )
```

profile of v0, /device:TPU:0, one launch (start us, length us, event | category | flops | bytes accessed | tf_op | source)
XLA Modules:
  0.0 1161.4 jit_solution(1971192605885689032)
XLA Ops:
  30.7 4.7 collective-permute-start
  44.8 21.7 %all-gather.6 = f32[8,1,24]{2,1,0:T(1,128)S(1)} all-gather(f32[1,1,24]{2,1,0:T(1,128)S(1)} %copy-done.327), channel_id=1, replica_groups=mesh['section'=2,'shard'=2,'dp'=8] {'dp'}, dimensions={0}, use_global_device_ids=true | all-gather | bytes 864 | tf_op jit(solution)/shard_map/all_gather | solution.py:26
  71.5 4.1 fusion.102
  75.6 65.2 %all-gather.28.cloned.1.call-done = f32[192,64,128]{2,1,0:T(8,128)} async-done(((f32[24,64,128]{2,1,0:T(8,128)}), f32[192,64,128]{2,1,0:T(8,128)}) %all-gather.28.cloned.1.call-update) | async-done | bytes 6291472 | tf_op jit(solution)/shard_map/all_gather | solution.py:26
  140.8 11.0 while.87
  207.8 18.0 %all-gather.7 = f32[8,1,24]{2,1,0:T(1,128)} all-gather(f32[1,1,24]{2,1,0:T(1,128)} %get-tuple-element.932), channel_id=1, replica_groups=mesh['section'=2,'shard'=2,'dp'=8] {'dp'}, dimensions={0}, use_global_device_ids=true | all-gather | bytes 864 | tf_op jit(solution)/shard_map/all_gather | solution.py:26
  233.9 5.2 fusion.105
  239.1 53.0 %all-gather.30.cloned.1.call-done = f32[192,64,128]{2,1,0:T(8,128)} async-done(((f32[24,64,128]{2,1,0:T(8,128)}), f32[192,64,128]{2,1,0:T(8,128)}) %all-gather.30.cloned.1.call-update) | async-done | bytes 6291472 | tf_op jit(solution)/shard_map/all_gather | solution.py:26
  292.1 28.7 %while.88 = (s32[]{:T(128)}, f32[24,64,128]{2,1,0:T(8,128)}, s32[]{:T(128)}, f32[8,24]{1,0:T(8,128)}, f32[8,24,64,128]{3,2,1,0:T(8,128)}, /*index=5*/s32[]{:T(128)}, s32[]{:T(128)}) while((s32[]{:T(128)}, f32[24,64,128]{2,1,0:T(8,128)}, s32[]{:T(128)}, f32[8,24]{1,0:T(8,128)}, f32[8,24,64,128]{3,2,1,0:T(8,128)}, ...), condition=%wide.region_12.13_spmd.clone, body=%wide.region_11.12_spmd.clone.sunk | while | flops 786436 | bytes 2359689 | solution.py:38
  328.7 4.2 fusion.144
  356.8 17.6 %all-gather.9 = bf16[8,1,24]{2,1,0:T(2,128)(2,1)S(1)} all-gather(bf16[1,1,24]{2,1,0:T(2,128)(2,1)S(1)} %bitcast.622), channel_id=1, replica_groups=mesh['section'=2,'shard'=2,'dp'=8] {'dp'}, dimensions={0}, use_global_device_ids=true | all-gather | bytes 432 | tf_op jit(solution)/shard_map/all_gather | solution.py:46
  381.5 4.5 collective-permute-start.3
  388.3 4.1 fusion.201
  398.5 6.8 all-gather.34.cloned.1.call-done
  405.4 13.9 %while.84 = (s32[]{:T(128)}, f32[24,64,128]{2,1,0:T(8,128)S(1)}, s32[]{:T(128)}, bf16[8,24]{1,0:T(8,128)(2,1)}, bf16[8,24,64,128]{3,2,1,0:T(8,128)(2,1)}, /*index=5*/s32[]{:T(128)}, s32[]{:T(128)}, s32[]{:T(128)}, s32[]{:T(128)}) while((s32[]{:T(128)}, f32[24,64,128]{2,1,0:T(8,128)S(1)}, s32[]{:T(128)}, bf16[8,24]{1,0:T(8,128)(2,1)}, ...), condition=%wide.region_26.28_spmd, body=%wide.region_25.27_spmd.sunk | while | flops 589854 | bytes 1966467 | solution.py:63
  434.6 4.2 multiply_reduce_fusion.14
  485.1 18.4 %all-gather.8 = f32[8,1,24]{2,1,0:T(1,128)} all-gather(f32[1,1,24]{2,1,0:T(1,128)} %get-tuple-element.928), channel_id=1, replica_groups=mesh['section'=2,'shard'=2,'dp'=8] {'dp'}, dimensions={0}, use_global_device_ids=true | all-gather | bytes 864 | tf_op jit(solution)/shard_map/all_gather | solution.py:26
  505.9 4.2 multiply_convert_fusion.2
  521.9 48.5 %all-gather.32.cloned.1.call-done = f32[192,64,128]{2,1,0:T(8,128)} async-done(((f32[24,64,128]{2,1,0:T(8,128)}), f32[192,64,128]{2,1,0:T(8,128)}) %all-gather.32.cloned.1.call-update) | async-done | bytes 6291472 | tf_op jit(solution)/shard_map/all_gather | solution.py:26
  570.4 28.7 %while.89 = (s32[]{:T(128)}, f32[24,64,128]{2,1,0:T(8,128)}, s32[]{:T(128)}, f32[8,24]{1,0:T(8,128)}, f32[8,24,64,128]{3,2,1,0:T(8,128)}, /*index=5*/s32[]{:T(128)}, s32[]{:T(128)}) while((s32[]{:T(128)}, f32[24,64,128]{2,1,0:T(8,128)}, s32[]{:T(128)}, f32[8,24]{1,0:T(8,128)}, f32[8,24,64,128]{3,2,1,0:T(8,128)}, ...), condition=%wide.region_19.20_spmd.clone, body=%wide.region_18.19_spmd.clone.sunk | while | flops 786436 | bytes 2359689 | solution.py:38
  603.7 4.2 fusion.150
  610.3 3.5 multiply_reduce_fusion.34
  618.2 4.2 fusion.138
  624.6 5.1 multiply_reduce_fusion.27
  641.1 17.8 %all-gather.10 = bf16[8,1,24]{2,1,0:T(2,128)(2,1)S(1)} all-gather(bf16[1,1,24]{2,1,0:T(2,128)(2,1)S(1)} %bitcast.623), channel_id=1, replica_groups=mesh['section'=2,'shard'=2,'dp'=8] {'dp'}, dimensions={0}, use_global_device_ids=true | all-gather | bytes 432 | tf_op jit(solution)/shard_map/all_gather | solution.py:46
  661.7 4.4 fusion.108
  674.8 4.1 fusion.203
  685.0 6.5 all-gather.36.cloned.1.call-done
  691.6 13.9 %while.85 = (s32[]{:T(128)}, f32[24,64,128]{2,1,0:T(8,128)S(1)}, s32[]{:T(128)}, bf16[8,24]{1,0:T(8,128)(2,1)}, bf16[8,24,64,128]{3,2,1,0:T(8,128)(2,1)}, /*index=5*/s32[]{:T(128)}, s32[]{:T(128)}, s32[]{:T(128)}, s32[]{:T(128)}) while((s32[]{:T(128)}, f32[24,64,128]{2,1,0:T(8,128)S(1)}, s32[]{:T(128)}, bf16[8,24]{1,0:T(8,128)(2,1)}, ...), condition=%wide.region_42.44_spmd, body=%wide.region_41.43_spmd.sunk | while | flops 589854 | bytes 1966467 | solution.py:63
  720.8 4.3 multiply_reduce_fusion.10
  746.6 6.4 collective-permute-done.8
  763.5 18.9 %all-gather.11 = bf16[8,1,24]{2,1,0:T(2,128)(2,1)S(1)} all-gather(bf16[1,1,24]{2,1,0:T(2,128)(2,1)S(1)} %bitcast.624), channel_id=1, replica_groups=mesh['section'=2,'shard'=2,'dp'=8] {'dp'}, dimensions={0}, use_global_device_ids=true | all-gather | bytes 432 | tf_op jit(solution)/shard_map/all_gather | solution.py:46
  786.3 4.1 fusion.205
  795.4 24.7 %all-gather.38.cloned.1.call-done = bf16[192,64,128]{2,1,0:T(8,128)(2,1)} async-done(((bf16[24,64,128]{2,1,0:T(8,128)(2,1)}), bf16[192,64,128]{2,1,0:T(8,128)(2,1)}) %all-gather.38.cloned.1.call-update) | async-done | bytes 3145744 | tf_op jit(solution)/shard_map/all_gather | solution.py:46
  820.2 13.4 %while.86 = (s32[]{:T(128)}, f32[24,64,128]{2,1,0:T(8,128)S(1)}, s32[]{:T(128)}, bf16[8,24]{1,0:T(8,128)(2,1)}, bf16[8,24,64,128]{3,2,1,0:T(8,128)(2,1)}, /*index=5*/s32[]{:T(128)}, s32[]{:T(128)}, s32[]{:T(128)}, s32[]{:T(128)}) while((s32[]{:T(128)}, f32[24,64,128]{2,1,0:T(8,128)S(1)}, s32[]{:T(128)}, bf16[8,24]{1,0:T(8,128)(2,1)}, ...), condition=%wide.region_59.61_spmd, body=%wide.region_58.60_spmd.sunk | while | flops 589854 | bytes 1966467 | solution.py:63
  849.0 4.1 multiply_reduce_fusion.6
  863.2 13.9 %convolution_convert_fusion = bf16[768,3352]{0,1:T(8,128)(2,1)S(1)} fusion(bf16[128,24]{1,0:T(8,128)(2,1)S(1)} %get-tuple-element.846, bf16[128,1792]{1,0:T(8,128)(2,1)S(1)} %fusion.212, bf16[128,1536]{1,0:T(8,128)(2,1)S(1)} %copy-done.102, bf16[128,24]{1,0:T(8,128)(2,1)} %copy-done.171, bf16[128,1792]{1,0:T(8,128)(2,1)S(1)} %copy-done.88, ...), kind=kOutput, calls=%fused_computation.15 | convolution fusion | flops 2004602880 | bytes 8312832 | tf_op jit(solution)/shard_map/dot_general | solution.py:80
  881.0 12.1 %copy.596 = bf16[1,768,1536]{2,0,1:T(2,128)(2,1)} copy(bf16[1,768,1536]{1,2,0:T(8,128)(2,1)} %slice_bitcast_fusion.1) | data formatting | bytes 4718592
  893.1 4.3 copy.629
  897.5 3.5 slice_bitcast_fusion
  901.0 12.7 %copy.598 = bf16[1,768,1792]{2,0,1:T(2,128)(2,1)} copy(bf16[1,768,1792]{1,2,0:T(8,128)(2,1)} %slice_bitcast_fusion) | data formatting | bytes 5505024
  913.7 4.5 copy.628
  954.4 4.3 copy.597
  961.5 4.5 copy.599
  979.6 5.8 reduce-scatter.36.cloned.1.call-done
  987.1 9.1 reduce-scatter.34.cloned.1.call-done
  997.3 39.7 %all-reduce.39 = (bf16[1,384]{1,0:T(2,128)(2,1)S(1)}, bf16[1,384,24]{1,2,0:T(8,128)(2,1)S(1)}, bf16[1,4,896]{2,1,0:T(4,128)(2,1)S(1)}, bf16[1,896]{1,0:T(2,128)(...) all-reduce(bf16[1,384]{1,0:T(2,128)(2,1)S(1)} %copy.595, ...), channel_id=1, replica_groups=mesh['section'=2,'shard'=2,'dp'=8] {'dp'}, use_global_device_ids=true, to_apply=%region_76.78 | all-reduce | flops 14884 | bytes 59536 | tf_op jit(solution)/shard_map/psum | solution.py:422
  1041.5 106.2 %all-reduce.45.cloned.1.call-done = (bf16[1,384,1536]{1,2,0:T(8,128)(2,1)}, bf16[1,384,1792]{1,2,0:T(8,128)(2,1)}, bf16[1,768,768]{2,1,0:T(8,128)(2,1)}) async-done(((bf16[1,384,1536]{1,2,0:T(8,128)(2,1)}, bf16[1,384,1792]{1,2,0:T(8,128)(2,1)}, bf16[1,768,768]{2,1,0:T(8,128)(2,1)}), (bf16[1,384,1536]{1,2,0:T(8,128)(2,1)}, bf16[1,384,1792]{1,2,0:T(8,128)(2,1)}, ...) | async-done | bytes 3735568 | tf_op jit(solution)/shard_map/psum | solution.py:423
  (1188 shorter events, 514.1 us)
Async XLA Ops:
  7.3 21.0 %all-gather.22.cloned.1.call-start = ((), (), s32[]{:S(2)}) async-start(), calls=%async_computation.8 | async-start | bytes 4128768 | tf_op jit(solution)/shard_map/all_gather | solution.py:327
  8.0 61.1 %all-gather.24.cloned.1.call-start = ((), (), s32[]{:S(2)}) async-start(), calls=%async_computation.9 | async-start | bytes 3538944 | tf_op jit(solution)/shard_map/all_gather | solution.py:326
  8.8 132.1 %all-gather.28.cloned.1.call-start = ((), (), s32[]{:S(2)}) async-start(), calls=%async_computation.12 | async-start | bytes 7077888 | tf_op jit(solution)/shard_map/all_gather | solution.py:26
  11.0 58.2 %copy-start.144 = (f32[768]{0:T(1024)}, f32[768]{0:T(1024)S(1)}, u32[]{:S(2)}) copy-start(f32[768]{0:T(1024)S(1)} %convert_reduce_fusion.5) | copy-start | bytes 9220
  12.2 28.7 %copy-start.229 = (s32[131]{0:T(256)}, s32[131]{0:T(256)S(1)}, u32[]{:S(2)}) copy-start(s32[131]{0:T(256)S(1)} %get-tuple-element.751) | copy-start | bytes 1576
  30.7 6.1 collective-permute-start
  38.1 28.5 %copy-start.157 = (f32[128,24]{1,0:T(8,128)S(1)}, f32[128,24]{1,0:T(8,128)}, u32[]{:S(2)}) copy-start(f32[128,24]{1,0:T(8,128)} %get-tuple-element.933) | copy-start | bytes 36868
  38.1 28.5 %copy-start.345 = (bf16[24]{0:T(256)(128)(2,1)S(1)}, bf16[24]{0:T(256)(128)(2,1)}, u32[]{:S(2)}) copy-start(bf16[24]{0:T(256)(128)(2,1)} %get-tuple-element.830) | copy-start | bytes 148
  38.2 28.5 %copy-start.308 = (bf16[1,768]{1,0:T(2,128)(2,1)S(1)}, bf16[1,768]{1,0:T(2,128)(2,1)}, u32[]{:S(2)}) copy-start(bf16[1,768]{1,0:T(2,128)(2,1)} %param.39) | copy-start | bytes 4612
  38.2 31.0 %copy-start.304 = (f32[128]{0:T(128)S(1)}, f32[128]{0:T(128)}, u32[]{:S(2)}) copy-start(f32[128]{0:T(128)} %copy-done.303) | copy-start | bytes 1540
  39.6 118.2 %all-gather.26.cloned.1.call-start = ((), (), s32[]{:S(2)}) async-start(), calls=%async_computation.10 | async-start | bytes 3538944 | tf_op jit(solution)/shard_map/all_gather | solution.py:335
  40.2 251.9 %all-gather.30.cloned.1.call-start = ((), (), s32[]{:S(2)}) async-start(), calls=%async_computation.13 | async-start | bytes 7077888 | tf_op jit(solution)/shard_map/all_gather | solution.py:26
  40.9 30.5 %copy-start.248 = (s32[131]{0:T(256)}, s32[131]{0:T(256)S(1)}, u32[]{:S(2)}) copy-start(s32[131]{0:T(256)S(1)} %get-tuple-element.954) | copy-start | bytes 1576
  66.7 85.1 %copy-start.232 = (f32[24]{0:T(128)}, f32[24]{0:T(128)S(1)}, u32[]{:S(2)}) copy-start(f32[24]{0:T(128)S(1)} %convert_element_type.774) | copy-start | bytes 292
  71.4 84.7 %copy-start.31 = (f32[128,1536]{1,0:T(8,128)}, f32[128,1536]{1,0:T(8,128)S(1)}, u32[]{:S(2)}) copy-start(f32[128,1536]{1,0:T(8,128)S(1)} %fusion.64) | copy-start | bytes 2359300
  151.8 169.0 %copy-start.8 = (f32[24,64,128]{2,1,0:T(8,128)}, f32[24,64,128]{2,1,0:T(8,128)S(1)}, u32[]{:S(2)}) copy-start(f32[24,64,128]{2,1,0:T(8,128)S(1)} %get-tuple-element.553) | copy-start | bytes 2359300
  160.4 6.9 collective-permute-start.1
  170.6 10.8 collective-permute-start.2
  192.8 212.5 %all-gather.34.cloned.1.call-start = ((), (), s32[]{:S(2)}) async-start(), calls=%async_computation.15 | async-start | bytes 3538944 | tf_op jit(solution)/shard_map/all_gather | solution.py:46
  344.3 49.9 %copy-start.14 = (f32[128,1536]{0,1:T(8,128)}, f32[128,1536]{0,1:T(8,128)S(1)}, u32[]{:S(2)}) copy-start(f32[128,1536]{0,1:T(8,128)S(1)} %copy.519) | copy-start | bytes 2359300
  346.4 224.0 %all-gather.32.cloned.1.call-start = ((), (), s32[]{:S(2)}) async-start(), calls=%async_computation.14 | async-start | bytes 7077888 | tf_op jit(solution)/shard_map/all_gather | solution.py:26
  348.9 30.3 %copy-start.2 = (bf16[1,1536,768]{2,1,0:T(8,128)(2,1)S(1)}, bf16[1,1536,768]{2,1,0:T(8,128)(2,1)}, u32[]{:S(2)}) copy-start(bf16[1,1536,768]{2,1,0:T(8,128)(2,1)} %all-gather.26.cloned.1.call-done) | copy-start | bytes 7077892
  381.5 68.6 %collective-permute-start.3 = (bf16[128,768]{1,0:T(8,128)(2,1)}, bf16[128,768]{1,0:T(8,128)(2,1)}, u32[]{:S(2)}, u32[]{:S(2)}) collective-permute-start(bf16[128,768]{1,0:T(8,128)(2,1)} %fusion.188), channel_id=1, source_target_pairs={{0,16},{1,17},{2,18},{3,19},{4,20},{5,21},{6,22},{7,23},{8,24},{9,... | collective-permute-start | bytes 589832 | tf_op jit(solution)/shard_map/ppermute | solution.py:21
  440.7 5.8 collective-permute-start.5
  453.7 5.7 collective-permute-start.4
  472.3 219.3 %all-gather.36.cloned.1.call-start = ((), (), s32[]{:S(2)}) async-start(), calls=%async_computation.16 | async-start | bytes 3538944 | tf_op jit(solution)/shard_map/all_gather | solution.py:46
  477.1 33.0 %copy-start.110 = (bf16[128,768]{1,0:T(8,128)(2,1)}, bf16[128,768]{1,0:T(8,128)(2,1)S(1)}, u32[]{:S(2)}) copy-start(bf16[128,768]{1,0:T(8,128)(2,1)S(1)} %fusion.344) | copy-start | bytes 589828
  477.1 43.1 %collective-permute-start.6 = (bf16[128,768]{1,0:T(8,128)(2,1)S(1)}, bf16[128,768]{1,0:T(8,128)(2,1)}, u32[]{:S(2)}, u32[]{:S(2)}) collective-permute-start(bf16[128,768]{1,0:T(8,128)(2,1)S(1)} %fusion.344), channel_id=1, source_target_pairs={{16,0},{17,1},{18,2},{19,3},{20,4},{21,5},{22,6},{23,7},{24,8},{25... | collective-permute-start | bytes 589832 | tf_op jit(solution)/shard_map/ppermute | solution.py:21
  479.6 26.3 %copy-start.118 = (f32[128,24]{0,1:T(8,128)}, f32[128,24]{0,1:T(8,128)S(1)}, u32[]{:S(2)}) copy-start(f32[128,24]{0,1:T(8,128)S(1)} %copy.509) | copy-start | bytes 36868
  482.9 23.0 %copy-start.116 = (f32[128,24]{0,1:T(8,128)}, f32[128,24]{0,1:T(8,128)S(1)}, u32[]{:S(2)}) copy-start(f32[128,24]{0,1:T(8,128)S(1)} %copy.553) | copy-start | bytes 36868
  570.4 28.7 %copy-start.9 = (f32[24,64,128]{2,1,0:T(8,128)S(1)}, f32[24,64,128]{2,1,0:T(8,128)}, u32[]{:S(2)}) copy-start(f32[24,64,128]{2,1,0:T(8,128)} %copy-done.8) | copy-start | bytes 2359300
  631.1 49.6 %copy-start.16 = (f32[128,1536]{0,1:T(8,128)}, f32[128,1536]{0,1:T(8,128)S(1)}, u32[]{:S(2)}) copy-start(f32[128,1536]{0,1:T(8,128)S(1)} %copy.534) | copy-start | bytes 2359300
  633.2 187.0 %all-gather.38.cloned.1.call-start = ((), (), s32[]{:S(2)}) async-start(), calls=%async_computation.17 | async-start | bytes 3538944 | tf_op jit(solution)/shard_map/all_gather | solution.py:46
  727.4 11.3 collective-permute-start.7
  745.3 7.7 collective-permute-start.8
  759.1 33.6 %copy-start.18 = (f32[128,1536]{0,1:T(8,128)}, f32[128,1536]{0,1:T(8,128)S(1)}, u32[]{:S(2)}) copy-start(f32[128,1536]{0,1:T(8,128)S(1)} %copy.556) | copy-start | bytes 2359300
  761.3 190.7 %reduce-scatter.30.cloned.1.call-start = ((), (), s32[]{:S(2)}) async-start(), calls=%async_computation.19 | async-start | bytes 3538944
  762.5 22.4 %copy-start.21 = (f32[24,64,128]{2,1,0:T(8,128)S(1)}, f32[24,64,128]{2,1,0:T(8,128)}, u32[]{:S(2)}) copy-start(f32[24,64,128]{2,1,0:T(8,128)} %get-tuple-element.907) | copy-start | bytes 2359300
  762.5 22.4 %copy-start.179 = (f32[128,24]{0,1:T(8,128)S(1)}, f32[128,24]{0,1:T(8,128)}, u32[]{:S(2)}) copy-start(f32[128,24]{0,1:T(8,128)} %exponential_multiply_fusion.6) | copy-start | bytes 36868
  855.5 6.4 collective-permute-start.9
  897.4 61.3 %reduce-scatter.32.cloned.1.call-start = ((), (), s32[]{:S(2)}) async-start(), calls=%async_computation.20 | async-start | bytes 4128768
  918.2 47.8 %reduce-scatter.26.cloned.1.call-start = ((), (), s32[]{:S(2)}) async-start(), calls=%async_computation.11 | async-start | bytes 3538944 | tf_op jit(solution)/shard_map/reduce_scatter | solution.py:417
  924.5 46.6 %reduce-scatter.40.cloned.1.call-start = ((), (), s32[]{:S(2)}) async-start(), calls=%async_computation.24 | async-start | bytes 589824
  931.5 43.3 %reduce-scatter.38.cloned.1.call-start = ((), (), s32[]{:S(2)}) async-start(), calls=%async_computation.23 | async-start | bytes 688128
  942.5 36.2 %reduce-scatter.28.cloned.1.call-start = ((), (), s32[]{:S(2)}) async-start(), calls=%async_computation.18 | async-start | bytes 294912
  946.9 38.4 %reduce-scatter.36.cloned.1.call-start = ((), (), s32[]{:S(2)}) async-start(), calls=%async_computation.22 | async-start | bytes 688128
  949.9 46.3 %reduce-scatter.34.cloned.1.call-start = ((), (), s32[]{:S(2)}) async-start(), calls=%async_computation.21 | async-start | bytes 294912
  951.8 195.8 %all-reduce.45.cloned.1.call-start = ((), (), s32[]{:S(2)}) async-start(), calls=%async_computation.25 | async-start | bytes 7471104 | tf_op jit(solution)/shard_map/psum | solution.py:423
  (326 other events, 1396.9 us)
Sparse Core Ops, SparseCore 0:
  9.7 14.2 all-gather.21
  25.5 12.1 all-gather.23
  40.4 100.3 all-gather.27
  142.2 9.1 all-gather.25
  192.9 99.1 all-gather.29
  346.5 58.8 all-gather.33
  472.4 97.9 all-gather.31
  633.3 58.1 all-gather.35
  761.4 58.7 all-gather.37
  897.5 7.9 reduce-scatter.29
  918.3 8.3 reduce-scatter.31
  929.4 11.2 reduce-scatter.25
  942.9 8.9 reduce-scatter.39
  954.1 9.0 reduce-scatter.37
  965.3 8.7 reduce-scatter.27
  976.3 9.0 reduce-scatter.35
  987.4 8.7 reduce-scatter.33
  1000.6 147.0 all-reduce.44
where the time goes:
time: 1180 us; the launch traced here: 1160 us
  waiting for transfers between devices  340 us (29%)
  other arithmetic  241 us (20%)
  local copies, waits for them, and re-layouts  186 us (16%)
  matrix products  170 us (14%)
  blocking collectives  167 us (14%)
  between operations  28 us (2%)
  starting transfers between devices  27.2 us (2%)
    all_gather x3, waiting for transfers between devices, entering(): everything = jax.tree.map(lambda part: lax.all_gather(part, axis), array)  167 us
    psum x1, waiting for transfers between devices, per_device(): lax.psum(totals[1].astype(jnp.bfloat16), 'dp').astype(jnp.float32)  106 us
    unnamed x729, local copies, waits for them, and re-layouts  81.3 us
    all_gather x3, blocking collectives, entering(): everything = jax.tree.map(lambda part: lax.all_gather(part, axis), array)  58 us
    all_gather x3, blocking collectives, carried_in(): lax.all_gather(a.astype(kind), axis)  54.3 us
    select_n x24, other arithmetic, turn(): return jax.tree.map(lambda a, b: jnp.where(reached, a, b), new, before)  48.9 us
    dot_general x12, matrix products, mix_out(): jnp.einsum('hij,jhp->ihp', weight * inner_cb[None], scaled, precision=hig...  46.9 us
    psum x1, blocking collectives, per_device(): lax.psum(totals[0].astype(jnp.bfloat16), 'dp').astype(jnp.float32)  39.7 us
  transfers between devices with their start and end apart: 28, of which 14 were waited for; matrix products, arithmetic and copies ran while one was open for 27% of the time, Pallas kernels for 0%

commit v1 on v0

--- a/solution.py
+++ b/solution.py
@@ -12,7 +12,7 @@
 
 
 epsilon = 1e-05
-highest = lax.Precision.HIGHEST
+high = lax.Precision.HIGH
 
 
 def passed_along(value, axis, steps):
@@ -21,46 +21,78 @@
     return lax.ppermute(value, axis, [(source, source + steps) for source in range(first, last)])
 
 
-def entering(array, axis, combine, identity):
-    size, here = (lax.axis_size(axis), lax.axis_index(axis))
-    everything = jax.tree.map(lambda part: lax.all_gather(part, axis), array)
-    start = jax.tree.map(
-        lambda part, zero: jnp.broadcast_to(jnp.asarray(zero, part.dtype), part.shape),
-        array,
-        identity,
-    )
-
-    def turn(k, before):
-        reached = k < here
-        new = combine(before, jax.tree.map(lambda part: part[k], everything))
-        return jax.tree.map(lambda a, b: jnp.where(reached, a, b), new, before)
-
-    return lax.fori_loop(0, size, turn, start)
-
-
-def carried_in(array, axis, join, neutral):
-    count = lax.axis_size(axis)
-    place = lax.axis_index(axis)
-    ahead = count - 1 - place
-    gathered = jax.tree.map(
-        lambda a, kind: lax.all_gather(a.astype(kind), axis),
-        array,
-        jax.tree.map(lambda a: jnp.bfloat16 if a.dtype == jnp.float32 else a.dtype, array),
-    )
-    state = jax.tree.map(lambda a, e: jnp.zeros_like(a) + jnp.asarray(e, a.dtype), array, neutral)
-
-    def one(turn, state):
-        source = count - 1 - turn
-        return join(
-            state,
-            jax.tree.map(
-                lambda a, own: lax.dynamic_index_in_dim(a, source, 0, False).astype(own.dtype),
-                gathered,
-                array,
-            ),
-        )
-
-    return lax.fori_loop(0, ahead, one, state)
+def spans(through_all, upward):
+    count, here = (lax.axis_size("dp"), lax.axis_index("dp"))
+    spot = jnp.arange(count, dtype=jnp.int32)
+    far, mid = (spot[:, None], spot[None, :])
+    if upward:
+        between, reached = ((mid > here) & (mid < far), spot > here)
+    else:
+        between, reached = ((mid < here) & (mid > far), spot < here)
+    factor = jnp.prod(jnp.where(between[:, :, None], through_all[None], 1.0), axis=1)
+    return jnp.where(reached[:, None], factor, 0.0)
+
+
+def weighted(states, factor):
+    return jnp.sum(states.astype(jnp.float32) * factor[:, :, None, None], axis=0)
+
+
+def entering(through, fresh_state):
+    count = lax.axis_size("dp")
+    coarse = lax.reduce_precision(through, 8, 7)
+    fine = through - coarse
+    decays = jnp.pad(jnp.stack([coarse, fine]), ((0, 14), (0, N - H)))
+    payload = jnp.concatenate([fresh_state.reshape(H * P_SIZE, N), decays], axis=0)
+    everything = lax.all_gather(payload.astype(jnp.bfloat16), "dp")
+    states = everything[:, : H * P_SIZE].reshape(count, H, P_SIZE, N)
+    halves = everything[:, H * P_SIZE : H * P_SIZE + 2, :H].astype(jnp.float32)
+    through_all = halves[:, 0] + halves[:, 1]
+    return (weighted(states, spans(through_all, False)), through_all)
+
+
+def carried_in(grad_state, through_all):
+    count = lax.axis_size("dp")
+    everything = lax.all_gather(grad_state.reshape(H * P_SIZE, N).astype(jnp.bfloat16), "dp")
+    return weighted(everything.reshape(count, H, P_SIZE, N), spans(through_all, True))
+
+
+def to_owner(whole):
+    count = lax.axis_size("shard")
+    rows = whole.shape[0] // count
+    low = whole.astype(jnp.bfloat16)
+    if count != 2:
+        return lax.psum_scatter(low, "shard", scatter_dimension=0, tiled=True)
+    me = lax.axis_index("shard")
+    theirs = lax.dynamic_slice_in_dim(low, (1 - me) * rows, rows, 0)
+    own = lax.dynamic_slice_in_dim(low, me * rows, rows, 0)
+    got = lax.ppermute(theirs, "shard", [(0, 1), (1, 0)])
+    return (own.astype(jnp.float32) + got.astype(jnp.float32)).astype(jnp.bfloat16)
+
+
+def pack_small(smalls, rows):
+    count = lax.axis_size("shard")
+    parts = []
+    for member in smalls:
+        if member.ndim == 2:
+            taps, width = member.shape
+            member = member.reshape(taps, count, width // count).transpose(1, 0, 2)
+        parts.append(member.reshape(count, -1))
+    flat = jnp.concatenate(parts, axis=1)
+    width = -(-flat.shape[1] // rows)
+    flat = jnp.pad(flat, ((0, 0), (0, width * rows - flat.shape[1])))
+    return flat.reshape(count * rows, width)
+
+
+def unpack_small(own, smalls):
+    count = lax.axis_size("shard")
+    flat = own.reshape(-1)
+    start, parts = (0, [])
+    for member in smalls:
+        shape = member.shape[:-1] + (member.shape[-1] // count,)
+        size = member.size // count
+        parts.append(flat[start : start + size].reshape(shape))
+        start += size
+    return parts
 
 
 def rms_scale(values):
@@ -86,10 +118,6 @@
     return lax.dot_general(
         left, right, (((1,), (1,)), ((), ())), preferred_element_type=jnp.float32
     )
-
-
-def chain_join(earlier, later):
-    return (earlier[0] * later[0], later[0][:, None, None] * earlier[1] + later[1])
 
 
 def conv_gate(extended, dt_raw, conv_w, conv_b, dt_bias, decay_rate, seg_ext):
@@ -120,7 +148,7 @@
         jnp.float32
     )
     fresh_state = jnp.einsum(
-        "jhp,jn->hpn", scaled * tail_decay[:, :, None], b_vals, precision=highest
+        "jhp,jn->hpn", scaled * tail_decay[:, :, None], b_vals, precision=high
     )
     through = jnp.exp(cumul[-1]) * (last_seg == prior_seg).astype(jnp.float32)
     return (through, fresh_state)
@@ -138,12 +166,14 @@
     cumul_t = cumul.T
     log_gaps = cumul_t[:, :, None] - cumul_t[:, None, :]
     weight = jnp.where(keep_mask, jnp.exp(jnp.where(keep_mask, log_gaps, 0.0)), 0.0)
-    inner_cb = jnp.dot(c_vals, b_vals.T, precision=highest)
+    inner_cb = jnp.dot(
+        c_vals.astype(jnp.bfloat16), b_vals.astype(jnp.bfloat16).T, preferred_element_type=jnp.float32
+    )
     scaled = heads_x * dt_vals[:, :, None]
-    y_inner = jnp.einsum("hij,jhp->ihp", weight * inner_cb[None], scaled, precision=highest)
+    y_inner = jnp.einsum("hij,jhp->ihp", weight * inner_cb[None], scaled, precision=high)
     entry_decay = jnp.exp(cumul) * (own_seg == prior_seg)[:, None].astype(jnp.float32)
     y_state = (
-        jnp.einsum("in,hpn->ihp", c_vals, state_in, precision=highest) * entry_decay[:, :, None]
+        jnp.einsum("in,hpn->ihp", c_vals, state_in, precision=high) * entry_decay[:, :, None]
     )
     y_full = (y_inner + y_state + d_skip[None, :, None] * heads_x).reshape(tok_rows, DI)
     gated = y_full * jax.nn.silu(gate_z)
@@ -152,10 +182,6 @@
 
 def small_params(weights):
     return tuple((weights[index_no].astype(jnp.float32) for index_no in (0, 4, 5, 6, 7, 8, 9)))
-
-
-def start_state():
-    return (jnp.ones((H,), jnp.float32), jnp.zeros((H, P_SIZE, N), jnp.float32))
 
 
 def layer_forward(hidden, weights, seg_ext):
@@ -176,8 +202,7 @@
     )
     xs_vals, b_vals, c_vals = split_low(activated)
     through, fresh_state = block_state(xs_vals, b_vals, dt_vals, cumul, own_seg, prior_seg)
-    prefix = entering((through, fresh_state), "dp", chain_join, start_state())
-    state_in = prefix[1]
+    state_in, through_all = entering(through, fresh_state)
     normed = mix_out(
         xs_vals,
         b_vals,
@@ -193,22 +218,11 @@
     )
     out_low = normed.astype(jnp.bfloat16)
     result = hidden + jnp.dot(out_low, weights[10], preferred_element_type=jnp.float32)
-    return (result, (hidden, normed_low, gate_z, extended, dt_raw, state_in, out_low, seg_ext))
-
-
-def weight_grads(pieces):
-    left_norm, three_low, left_out, grad_low = pieces
-    wide = col_product(left_norm, three_low)
-    return (
-        wide[:, :DI],
-        wide[:, DI : DI + XC],
-        wide[:, DI + XC :],
-        col_product(left_out, grad_low),
-    )
+    return (result, (hidden, normed_low, gate_z, extended, dt_raw, state_in, out_low, seg_ext, through_all))
 
 
 def layer_back(grad_out, kept, weights, valid):
-    hidden, normed_low, gate_z, extended, dt_raw, state_in, out_low, seg_ext = kept
+    hidden, normed_low, gate_z, extended, dt_raw, state_in, out_low, seg_ext, through_all = kept
     gain_in, conv_wf, conv_bf, bias_f, rate_f, skip_f, ggain_f = small_params(weights)
     tok_rows = hidden.shape[0]
     own_seg = seg_ext[KW - 1 :]
@@ -250,8 +264,7 @@
         return block_state(xs_arg, b_arg, dt_arg, cum_arg, own_seg, prior_seg)
 
     (through, fresh_unused), state_back = jax.vjp(state_fn, xs_vals, b_vals, dt_vals, cumul)
-    suffix = carried_in((through, grad_state), "dp", chain_join, start_state())
-    later_grad = suffix[1]
+    later_grad = carried_in(grad_state, through_all)
     grad_through = jnp.sum(later_grad * state_in, axis=(1, 2))
     more_xs, more_b, more_dt, more_cum = state_back((grad_through, later_grad))
     grad_act = jnp.concatenate([grad_xs + more_xs, grad_b + more_b, grad_c], axis=1)
@@ -272,8 +285,8 @@
     value_unused, norm_back = jax.vjp(norm_in, hidden, gain_in)
     grad_hidden, grad_gain = norm_back(grad_normed_in)
     valid_low = valid.astype(jnp.bfloat16)
-    three_low = jnp.concatenate([gate_low, conv_low, step_low], axis=1)
-    pieces = (normed_low * valid_low, three_low, out_low * valid_low, grad_low)
+    two_low = jnp.concatenate([conv_low, step_low], axis=1)
+    pieces = (normed_low * valid_low, gate_low, two_low, out_low * valid_low, grad_low)
     smalls = tuple(
         (
             member * valid
@@ -281,22 +294,6 @@
         )
     )
     return (grad_hidden + grad_out, smalls, pieces)
-
-
-def full_grads(smalls, larges):
-    return (
-        smalls[0],
-        larges[0],
-        larges[1],
-        larges[2],
-        smalls[1],
-        smalls[2],
-        smalls[3],
-        smalls[4],
-        smalls[5],
-        smalls[6],
-        larges[3],
-    )
 
 
 def per_device(
@@ -378,59 +375,39 @@
     joined = tuple(
         (
             jnp.concatenate([piece[index_no] for piece in piece_steps], axis=0)
-            for index_no in range(4)
-        )
-    )
-    grads = full_grads(small_total, weight_grads(joined))
-    lifted = tuple((member[None] for member in grads))
+            for index_no in range(5)
+        )
+    )
+    left_norm, gate_all, two_all, left_out, grad_all = joined
+    own_out = lax.psum(to_owner(col_product(left_out, grad_all)), "dp")
+    gate_part = to_owner(col_product(left_norm, gate_all))
+    gate_part, own_out = lax.optimization_barrier((gate_part, own_out))
+    own_gate = lax.psum(gate_part, "dp")
+    small_rows = left_norm.shape[1] // lax.axis_size("shard")
+    rest_part = to_owner(
+        jnp.concatenate(
+            [col_product(left_norm, two_all), pack_small(small_total, small_rows)], axis=1
+        )
+    )
+    rest_part, own_gate = lax.optimization_barrier((rest_part, own_gate))
+    own_rest = lax.psum(rest_part, "dp").astype(jnp.float32)
+    gains, taps, biases, steps, rates, skips, ggains = unpack_small(
+        own_rest[:, XC + H :], small_total
+    )
     totals = (
-        lax.psum_scatter(
-            lifted[0].astype(jnp.bfloat16), "shard", scatter_dimension=1, tiled=True
-        ).astype(jnp.float32),
-        lax.psum_scatter(
-            lifted[1].astype(jnp.bfloat16), "shard", scatter_dimension=1, tiled=True
-        ).astype(jnp.float32),
-        lax.psum_scatter(
-            lifted[2].astype(jnp.bfloat16), "shard", scatter_dimension=1, tiled=True
-        ).astype(jnp.float32),
-        lax.psum_scatter(
-            lifted[3].astype(jnp.bfloat16), "shard", scatter_dimension=1, tiled=True
-        ).astype(jnp.float32),
-        lax.psum_scatter(
-            lifted[4].astype(jnp.bfloat16), "shard", scatter_dimension=2, tiled=True
-        ).astype(jnp.float32),
-        lax.psum_scatter(
-            lifted[5].astype(jnp.bfloat16), "shard", scatter_dimension=1, tiled=True
-        ).astype(jnp.float32),
-        lax.psum_scatter(
-            lifted[6].astype(jnp.bfloat16), "shard", scatter_dimension=1, tiled=True
-        ).astype(jnp.float32),
-        lax.psum_scatter(
-            lifted[7].astype(jnp.bfloat16), "shard", scatter_dimension=1, tiled=True
-        ).astype(jnp.float32),
-        lax.psum_scatter(
-            lifted[8].astype(jnp.bfloat16), "shard", scatter_dimension=1, tiled=True
-        ).astype(jnp.float32),
-        lax.psum_scatter(
-            lifted[9].astype(jnp.bfloat16), "shard", scatter_dimension=1, tiled=True
-        ).astype(jnp.float32),
-        lax.psum_scatter(
-            lifted[10].astype(jnp.bfloat16), "shard", scatter_dimension=1, tiled=True
-        ).astype(jnp.float32),
-    )
-    totals = (
-        lax.psum(totals[0].astype(jnp.bfloat16), "dp").astype(jnp.float32),
-        lax.psum(totals[1].astype(jnp.bfloat16), "dp").astype(jnp.float32),
-        lax.psum(totals[2].astype(jnp.bfloat16), "dp").astype(jnp.float32),
-        lax.psum(totals[3].astype(jnp.bfloat16), "dp").astype(jnp.float32),
-        lax.psum(totals[4].astype(jnp.bfloat16), "dp").astype(jnp.float32),
-        lax.psum(totals[5].astype(jnp.bfloat16), "dp").astype(jnp.float32),
-        lax.psum(totals[6].astype(jnp.bfloat16), "dp").astype(jnp.float32),
-        lax.psum(totals[7].astype(jnp.bfloat16), "dp").astype(jnp.float32),
-        lax.psum(totals[8].astype(jnp.bfloat16), "dp").astype(jnp.float32),
-        lax.psum(totals[9].astype(jnp.bfloat16), "dp").astype(jnp.float32),
-        lax.psum(totals[10].astype(jnp.bfloat16), "dp").astype(jnp.float32),
-    )
+        gains,
+        own_gate.astype(jnp.float32),
+        own_rest[:, :XC],
+        own_rest[:, XC : XC + H],
+        taps,
+        biases,
+        steps,
+        rates,
+        skips,
+        ggains,
+        own_out.astype(jnp.float32),
+    )
+    totals = tuple((member[None] for member in totals))
     activations = jnp.stack(
         [pick(sent_steps[micro_no], sent_steps[micro_no + 1]) for micro_no in range(micro)]
     )

time: 1180 us -> 963 us (0.82)
  blocking collectives: 167 us -> 12.1 us
  other arithmetic: 241 us -> 207 us
  matrix products: 170 us -> 143 us
    all_gather x6 -> x0, blocking collectives: 112 us -> none  [the longest x3 58 us: entering(): everything = jax.tree.map(lambda part: lax.all_gather(part, axis), array)]
    psum x1 -> x3, waiting for transfers between devices: 106 us -> 175 us  [the longest x1 84.2 us: per_device(): own_rest = lax.psum(rest_part, 'dp').astype(jnp.float32)]
    all_gather x6, waiting for transfers between devices: 205 us -> 144 us  [the longest x3 113 us: entering(): everything = lax.all_gather(payload.astype(jnp.bfloat16), 'dp')]
    unnamed x729 -> x645, local copies, waits for them, and re-layouts: 81.3 us -> 27.4 us
    select_n x24 -> x5, other arithmetic: 48.9 us -> 2.92 us  [spans(): return jnp.where(reached[:, None], factor, 0.0)]
    psum x1 -> x0, blocking collectives: 39.7 us -> none  [per_device(): lax.psum(totals[0].astype(jnp.bfloat16), 'dp').astype(jnp.float32)]
    reduce_sum x3 -> x9, other arithmetic: 4.57 us -> 29.9 us  [the longest x6 23.4 us: weighted(): jnp.sum(states.astype(jnp.float32) * factor[:, :, None, None], axis=0)]
    add x21 -> x1, other arithmetic: 25.1 us -> 0.01 us  [entering(): through_all = halves[:, 0] + halves[:, 1]]
  transfers between devices with their start and end apart: 28 -> 25, of which waited for: 14 -> 12; matrix products, arithmetic and copies ran while one was open for 27% -> 38% of each run, Pallas kernels for 0% -> 0%
where the time goes in v1:
time: 963 us; the launch traced here: 946 us
  waiting for transfers between devices  334 us (35%)
  other arithmetic  207 us (21%)
  local copies, waits for them, and re-layouts  194 us (20%)
  matrix products  143 us (15%)
  starting transfers between devices  30.2 us (3%)
  between operations  26.7 us (3%)
  blocking collectives  12.1 us (1%)
    all_gather x3, waiting for transfers between devices, entering(): everything = lax.all_gather(payload.astype(jnp.bfloat16), 'dp')  113 us
    psum x1, waiting for transfers between devices, per_device(): own_rest = lax.psum(rest_part, 'dp').astype(jnp.float32)  84.2 us
    psum x1, waiting for transfers between devices, per_device(): own_gate = lax.psum(gate_part, 'dp')  77.7 us
    dot_general x12, matrix products, mix_out(): jnp.einsum('hij,jhp->ihp', weight * inner_cb[None], scaled, precision=high)  37.8 us
    all_gather x3, waiting for transfers between devices, carried_in(): lax.all_gather(grad_state.reshape(H * P_SIZE, N).astype(jnp.bfloat16), 'dp')  31.5 us
    ppermute x10, starting transfers between devices, passed_along(): lax.ppermute(value, axis, [(source, source + steps) for source in range(f...  27.9 us
    unnamed x645, local copies, waits for them, and re-layouts  27.4 us
    reduce_sum x6, other arithmetic, weighted(): jnp.sum(states.astype(jnp.float32) * factor[:, :, None, None], axis=0)  23.4 us
  transfers between devices with their start and end apart: 25, of which 12 were waited for; matrix products, arithmetic and copies ran while one was open for 38% of the time, Pallas kernels for 0%

profile of v1, /device:TPU:0, one launch (start us, length us, event | category | flops | bytes accessed | tf_op | source)
XLA Modules:
  0.0 946.5 jit_solution(18122967803878383008)
XLA Ops:
  21.2 3.0 all-reduce.40
  30.3 4.7 collective-permute-start
  56.1 47.5 %all-gather.15.cloned.1.call-done = bf16[8,1552,128]{2,1,0:T(8,128)(2,1)} async-done(((bf16[1,1552,128]{2,1,0:T(8,128)(2,1)}), bf16[8,1552,128]{2,1,0:T(8,128)(2,1)}) %all-gather.15.cloned.1.call-update) | async-done | bytes 3178512 | tf_op jit(solution)/shard_map/all_gather | solution.py:46
  105.2 3.9 multiply_reduce_fusion.2
  111.5 3.0 all-gather.19.cloned.1.call-done
  117.0 3.6 collective-permute-start.1
  122.6 2.6 collective-permute-done.1
  128.6 3.7 collective-permute-start.2
  158.8 3.8 fusion.103
  162.6 46.7 %all-gather.21.cloned.1.call-done = bf16[8,1552,128]{2,1,0:T(8,128)(2,1)} async-done(((bf16[1,1552,128]{2,1,0:T(8,128)(2,1)}), bf16[8,1552,128]{2,1,0:T(8,128)(2,1)}) %all-gather.21.cloned.1.call-update) | async-done | bytes 3178512 | tf_op jit(solution)/shard_map/all_gather | solution.py:46
  211.9 3.9 multiply_reduce_fusion.1
  222.5 4.3 fusion.142
  229.1 3.0 multiply_reduce_fusion.44
  234.2 2.6 multiply_reduce_fusion.23
  248.8 2.7 compare_convert_fusion.15
  251.5 2.7 compare_convert_fusion
  272.6 3.7 collective-permute-start.3
  276.4 3.1 fusion.210
  286.9 15.2 %all-gather.25.cloned.1.call-done = bf16[12288,128]{1,0:T(8,128)(2,1)} async-done(((bf16[1536,128]{1,0:T(8,128)(2,1)}), bf16[12288,128]{1,0:T(8,128)(2,1)}) %all-gather.25.cloned.1.call-update) | async-done | bytes 3145744 | tf_op jit(solution)/shard_map/all_gather | solution.py:55
  302.2 3.9 fusion.2
  319.9 4.0 multiply_reduce_fusion.41
  357.0 5.1 collective-permute-start.4
  381.6 2.7 compare_convert_fusion.5
  404.9 4.2 multiply_convert_fusion.2
  422.3 18.5 %all-gather.23.cloned.1.call-done = bf16[8,1552,128]{2,1,0:T(8,128)(2,1)} async-done(((bf16[1,1552,128]{2,1,0:T(8,128)(2,1)}), bf16[8,1552,128]{2,1,0:T(8,128)(2,1)}) %all-gather.23.cloned.1.call-update) | async-done | bytes 3178512 | tf_op jit(solution)/shard_map/all_gather | solution.py:46
  447.3 3.9 multiply_reduce_fusion
  454.9 2.6 fusion.148
  459.9 3.7 multiply_reduce_fusion.37
  471.7 5.3 multiply_reduce_fusion.30
  500.8 2.9 fusion.106
  513.3 4.4 fusion.212
  525.4 16.3 %all-gather.27.cloned.1.call-done = bf16[12288,128]{1,0:T(8,128)(2,1)} async-done(((bf16[1536,128]{1,0:T(8,128)(2,1)}), bf16[12288,128]{1,0:T(8,128)(2,1)}) %all-gather.27.cloned.1.call-update) | async-done | bytes 3145744 | tf_op jit(solution)/shard_map/all_gather | solution.py:55
  541.7 3.9 fusion.1
  559.2 4.0 multiply_reduce_fusion.34
  593.0 6.6 collective-permute-done.8
  601.7 2.7 multiply_reduce_fusion.21
  655.3 4.3 fusion.214
  665.3 3.2 fusion.124
  671.8 2.6 add_convert_fusion.1
  674.8 3.9 fusion
  689.4 3.8 multiply_reduce_fusion.27
  733.2 3.3 convolution_convert_fusion
  739.1 3.2 add_convert_fusion.2
  742.3 13.4 %all-reduce.45.cloned.1.call-done = bf16[768,768]{1,0:T(8,128)(2,1)} async-done(((bf16[768,768]{1,0:T(8,128)(2,1)}), bf16[768,768]{1,0:T(8,128)(2,1)}) %all-reduce.45.cloned.1.call-update) | async-done | bytes 1179664 | tf_op jit(solution)/shard_map/psum | solution.py:382
  758.5 2.8 add_convert_fusion
  761.3 77.7 %all-reduce.47.cloned.1.call-done = bf16[384,1536]{1,0:T(8,128)(2,1)} async-done(((bf16[384,1536]{1,0:T(8,128)(2,1)}), bf16[384,1536]{1,0:T(8,128)(2,1)}) %all-reduce.47.cloned.1.call-update) | async-done | bytes 1179664 | tf_op jit(solution)/shard_map/psum | solution.py:385
  843.8 84.2 %all-reduce.49.cloned.1.call-done = bf16[384,1831]{0,1:T(8,128)(2,1)} async-done(((bf16[384,1831]{0,1:T(8,128)(2,1)}), bf16[384,1831]{0,1:T(8,128)(2,1)}) %all-reduce.49.cloned.1.call-update) | async-done | bytes 1406224 | tf_op jit(solution)/shard_map/psum | solution.py:393
  933.6 3.3 copy.650
  (1072 shorter events, 455.2 us)
Async XLA Ops:
  7.3 16.9 %copy-start.220 = (bf16[1,384,24]{1,2,0:T(8,128)(2,1)S(1)}, bf16[1,384,24]{1,2,0:T(8,128)(2,1)}, u32[]{:S(2)}) copy-start(bf16[1,384,24]{1,2,0:T(8,128)(2,1)} %param.21) | copy-start | bytes 55300
  7.3 20.6 %all-gather.13.cloned.1.call-start = ((), (), s32[]{:S(2)}) async-start(), calls=%async_computation | async-start | bytes 4128768 | tf_op jit(solution)/shard_map/all_gather | solution.py:324
  8.0 42.2 %all-gather.17.cloned.1.call-start = ((), (), s32[]{:S(2)}) async-start(), calls=%async_computation.2 | async-start | bytes 3538944 | tf_op jit(solution)/shard_map/all_gather | solution.py:323
  8.8 94.8 %all-gather.15.cloned.1.call-start = ((), (), s32[]{:S(2)}) async-start(), calls=%async_computation.1 | async-start | bytes 3575808 | tf_op jit(solution)/shard_map/all_gather | solution.py:46
  9.0 21.2 %copy-start.281 = (f32[128]{0:T(128)}, f32[128]{0:T(128)S(1)}, u32[]{:S(2)}) copy-start(f32[128]{0:T(128)S(1)} %add_rsqrt_fusion.5) | copy-start | bytes 1540
  11.0 19.3 %copy-start.154 = (f32[768]{0:T(1024)}, f32[768]{0:T(1024)S(1)}, u32[]{:S(2)}) copy-start(f32[768]{0:T(1024)S(1)} %convert_reduce_fusion.5) | copy-start | bytes 9220
  14.7 21.9 %copy-start.136 = (f32[1792]{0:T(1024)}, f32[1792]{0:T(1024)S(1)}, u32[]{:S(2)}) copy-start(f32[1792]{0:T(1024)S(1)} %get-tuple-element.162) | copy-start | bytes 21508
  14.7 21.9 %copy-start.142 = (f32[1792]{0:T(1024)}, f32[1792]{0:T(1024)S(1)}, u32[]{:S(2)}) copy-start(f32[1792]{0:T(1024)S(1)} %get-tuple-element.163) | copy-start | bytes 21508
  14.7 21.9 %copy-start.148 = (f32[1792]{0:T(1024)}, f32[1792]{0:T(1024)S(1)}, u32[]{:S(2)}) copy-start(f32[1792]{0:T(1024)S(1)} %get-tuple-element.164) | copy-start | bytes 21508
  30.3 6.1 collective-permute-start
  40.6 73.9 %all-gather.19.cloned.1.call-start = ((), (), s32[]{:S(2)}) async-start(), calls=%async_computation.3 | async-start | bytes 3538944 | tf_op jit(solution)/shard_map/all_gather | solution.py:332
  41.2 168.0 %all-gather.21.cloned.1.call-start = ((), (), s32[]{:S(2)}) async-start(), calls=%async_computation.4 | async-start | bytes 3575808 | tf_op jit(solution)/shard_map/all_gather | solution.py:46
  41.8 62.6 %copy-start.279 = (pred[8]{0:T(512)(128)(4,1)}, pred[8]{0:T(512)(128)(4,1)S(1)}, u32[]{:S(2)}) copy-start(pred[8]{0:T(512)(128)(4,1)S(1)} %get-tuple-element.361) | copy-start | bytes 28
  46.3 58.0 %copy-start.245 = (pred[8,8]{1,0:T(8,128)(4,1)}, pred[8,8]{1,0:T(8,128)(4,1)S(1)}, u32[]{:S(2)}) copy-start(pred[8,8]{1,0:T(8,128)(4,1)S(1)} %fusion.479) | copy-start | bytes 196
  52.5 58.1 %copy-start.31 = (f32[128,1536]{1,0:T(8,128)}, f32[128,1536]{1,0:T(8,128)S(1)}, u32[]{:S(2)}) copy-start(f32[128,1536]{1,0:T(8,128)S(1)} %fusion.46) | copy-start | bytes 2359300
  114.6 12.6 %copy-start = (bf16[1,768,1792]{2,1,0:T(8,128)(2,1)S(1)}, bf16[1,768,1792]{2,1,0:T(8,128)(2,1)}, u32[]{:S(2)}) copy-start(bf16[1,768,1792]{2,1,0:T(8,128)(2,1)} %all-gather.13.cloned.1.call-done) | copy-start | bytes 8257540
  117.0 8.2 collective-permute-start.1
  128.6 7.3 collective-permute-start.2
  140.0 18.0 %copy-start.49 = (bf16[128,1792]{1,0:T(8,128)(2,1)}, bf16[128,1792]{1,0:T(8,128)(2,1)S(1)}, u32[]{:S(2)}) copy-start(bf16[128,1792]{1,0:T(8,128)(2,1)S(1)} %get-tuple-element.217) | copy-start | bytes 1376260
  147.4 154.8 %all-gather.25.cloned.1.call-start = ((), (), s32[]{:S(2)}) async-start(), calls=%async_computation.9 | async-start | bytes 3538944 | tf_op jit(solution)/shard_map/all_gather | solution.py:55
  158.0 52.0 %copy-start.206 = (f32[8,1,24]{2,1,0:T(1,128)S(1)}, f32[8,1,24]{2,1,0:T(1,128)}, u32[]{:S(2)}) copy-start(f32[8,1,24]{2,1,0:T(1,128)} %copy-done.205) | copy-start | bytes 2308
  158.8 51.8 %copy-start.246 = (pred[8,8]{1,0:T(8,128)(4,1)S(1)}, pred[8,8]{1,0:T(8,128)(4,1)}, u32[]{:S(2)}) copy-start(pred[8,8]{1,0:T(8,128)(4,1)} %copy-done.245) | copy-start | bytes 196
  158.8 51.9 %copy-start.280 = (pred[8]{0:T(512)(128)(4,1)S(1)}, pred[8]{0:T(512)(128)(4,1)}, u32[]{:S(2)}) copy-start(pred[8]{0:T(512)(128)(4,1)} %copy-done.279) | copy-start | bytes 28
  243.2 197.7 %all-gather.23.cloned.1.call-start = ((), (), s32[]{:S(2)}) async-start(), calls=%async_computation.5 | async-start | bytes 3575808 | tf_op jit(solution)/shard_map/all_gather | solution.py:46
  272.6 77.0 %collective-permute-start.3 = (bf16[128,768]{1,0:T(8,128)(2,1)}, bf16[128,768]{1,0:T(8,128)(2,1)}, u32[]{:S(2)}, u32[]{:S(2)}) collective-permute-start(bf16[128,768]{1,0:T(8,128)(2,1)} %fusion.191), channel_id=1, source_target_pairs={{0,16},{1,17},{2,18},{3,19},{4,20},{5,21},{6,22},{7,23},{8,24},{9,... | collective-permute-start | bytes 589832 | tf_op jit(solution)/shard_map/ppermute | solution.py:21
  332.7 14.5 %collective-permute-start.5 = (f32[3,1792]{1,0:T(4,128)}, f32[3,1792]{1,0:T(4,128)}, u32[]{:S(2)}, u32[]{:S(2)}) collective-permute-start(f32[3,1792]{1,0:T(4,128)} %pad_add_fusion.5), channel_id=1, source_target_pairs={{1,0},{2,1},{3,2},{4,3},{5,4},{6,5},{7,6},{9,8},{10,9},{11,10},{12... | collective-permute-start | bytes 64520 | tf_op jit(solution)/shard_map/ppermute | solution.py:21
  357.0 9.6 %collective-permute-start.4 = (bf16[3,1792]{1,0:T(4,128)(2,1)}, bf16[3,1792]{1,0:T(4,128)(2,1)}, u32[]{:S(2)}, u32[]{:S(2)}) collective-permute-start(bf16[3,1792]{1,0:T(4,128)(2,1)} %slice.611), channel_id=1, source_target_pairs={{0,1},{1,2},{2,3},{3,4},{4,5},{5,6},{6,7},{8,9},{9,10},{10,11},{11... | collective-permute-start | bytes 32264 | tf_op jit(solution)/shard_map/ppermute | solution.py:21
  380.1 161.6 %all-gather.27.cloned.1.call-start = ((), (), s32[]{:S(2)}) async-start(), calls=%async_computation.10 | async-start | bytes 3538944 | tf_op jit(solution)/shard_map/all_gather | solution.py:55
  388.5 32.1 %collective-permute-start.6 = (bf16[128,768]{1,0:T(8,128)(2,1)}, bf16[128,768]{1,0:T(8,128)(2,1)}, u32[]{:S(2)}, u32[]{:S(2)}) collective-permute-start(bf16[128,768]{1,0:T(8,128)(2,1)} %fusion.342), channel_id=1, source_target_pairs={{16,0},{17,1},{18,2},{19,3},{20,4},{21,5},{22,6},{23,7},{24,8},{25... | collective-permute-start | bytes 589832 | tf_op jit(solution)/shard_map/ppermute | solution.py:21
  483.4 191.3 %all-gather.29.cloned.1.call-start = ((), (), s32[]{:S(2)}) async-start(), calls=%async_computation.11 | async-start | bytes 3538944 | tf_op jit(solution)/shard_map/all_gather | solution.py:55
  571.9 14.6 %collective-permute-start.7 = (f32[3,1792]{1,0:T(4,128)}, f32[3,1792]{1,0:T(4,128)}, u32[]{:S(2)}, u32[]{:S(2)}) collective-permute-start(f32[3,1792]{1,0:T(4,128)} %pad_add_fusion.4), channel_id=1, source_target_pairs={{1,0},{2,1},{3,2},{4,3},{5,4},{6,5},{7,6},{9,8},{10,9},{11,10},{12... | collective-permute-start | bytes 64520 | tf_op jit(solution)/shard_map/ppermute | solution.py:21
  591.7 7.9 collective-permute-start.8
  610.7 145.0 %all-reduce.45.cloned.1.call-start = ((), (), s32[]{:S(2)}) async-start(), calls=%async_computation.6 | async-start | bytes 2359296 | tf_op jit(solution)/shard_map/psum | solution.py:382
  645.9 25.4 %collective-permute-start.12 = (bf16[768,768]{1,0:T(8,128)(2,1)}, bf16[768,768]{1,0:T(8,128)(2,1)}, u32[]{:S(2)}, u32[]{:S(2)}) collective-permute-start(bf16[768,768]{1,0:T(8,128)(2,1)} %constant_dynamic-slice_fusion), channel_id=1, source_target_pairs={{0,8},{8,0},{1,9},{9,1},{2,10},{10,2},{3,11},{11,3},{4,12},{12,4},... | collective-permute-start | bytes 3538952 | tf_op jit(solution)/shard_map/ppermute | solution.py:68
  651.3 87.8 %collective-permute-start.11 = (bf16[384,1536]{1,0:T(8,128)(2,1)}, bf16[384,1536]{1,0:T(8,128)(2,1)}, u32[]{:S(2)}, u32[]{:S(2)}) collective-permute-start(bf16[384,1536]{1,0:T(8,128)(2,1)} %constant_dynamic-slice_fusion.1), channel_id=1, source_target_pairs={{0,8},{8,0},{1,9},{9,1},{2,10},{10,2},{3,11},{11,3},{4,12},{12,4},... | collective-permute-start | bytes 3538952 | tf_op jit(solution)/shard_map/ppermute | solution.py:68
  674.5 164.6 %all-reduce.47.cloned.1.call-start = ((), (), s32[]{:S(2)}) async-start(), calls=%async_computation.7 | async-start | bytes 2359296 | tf_op jit(solution)/shard_map/psum | solution.py:385
  701.7 27.7 %copy-start.30 = (bf16[128,768]{1,0:T(8,128)(2,1)S(1)}, bf16[128,768]{1,0:T(8,128)(2,1)}, u32[]{:S(2)}) copy-start(bf16[128,768]{1,0:T(8,128)(2,1)} %copy-done.27) | copy-start | bytes 589828
  701.7 27.7 %copy-start.46 = (bf16[128,768]{1,0:T(8,128)(2,1)S(1)}, bf16[128,768]{1,0:T(8,128)(2,1)}, u32[]{:S(2)}) copy-start(bf16[128,768]{1,0:T(8,128)(2,1)} %copy-done.44) | copy-start | bytes 589828
  701.7 27.7 %copy-start.116 = (f32[128,768]{1,0:T(8,128)S(1)}, f32[128,768]{1,0:T(8,128)}, u32[]{:S(2)}) copy-start(f32[128,768]{1,0:T(8,128)} %fusion.36) | copy-start | bytes 1179652
  701.7 27.7 %copy-start.160 = (f32[768]{0:T(1024)S(1)}, f32[768]{0:T(1024)}, u32[]{:S(2)}) copy-start(f32[768]{0:T(1024)} %copy-done.154) | copy-start | bytes 9220
  705.3 24.2 %copy-start.287 = (f32[128]{0:T(128)S(1)}, f32[128]{0:T(128)}, u32[]{:S(2)}) copy-start(f32[128]{0:T(128)} %fusion.489) | copy-start | bytes 1540
  715.0 13.1 %collective-permute-start.9 = (f32[3,1792]{1,0:T(4,128)}, f32[3,1792]{1,0:T(4,128)}, u32[]{:S(2)}, u32[]{:S(2)}) collective-permute-start(f32[3,1792]{1,0:T(4,128)} %pad_add_fusion.3), channel_id=1, source_target_pairs={{1,0},{2,1},{3,2},{4,3},{5,4},{6,5},{7,6},{9,8},{10,9},{11,10},{12... | collective-permute-start | bytes 64520 | tf_op jit(solution)/shard_map/ppermute | solution.py:21
  738.6 19.9 %collective-permute-start.10 = (bf16[384,1831]{0,1:T(8,128)(2,1)}, bf16[384,1831]{0,1:T(8,128)(2,1)}, u32[]{:S(2)}, u32[]{:S(2)}) collective-permute-start(bf16[384,1831]{0,1:T(8,128)(2,1)} %fusion.98), channel_id=1, source_target_pairs={{0,8},{8,0},{1,9},{9,1},{2,10},{10,2},{3,11},{11,3},{4,12},{12,4},... | collective-permute-start | bytes 4218632 | tf_op jit(solution)/shard_map/ppermute | solution.py:68
  739.1 16.9 %copy-start.128 = (bf16[128,768]{1,0:T(8,128)(2,1)S(1)}, bf16[128,768]{1,0:T(8,128)(2,1)}, u32[]{:S(2)}) copy-start(bf16[128,768]{1,0:T(8,128)(2,1)} %copy-done.127) | copy-start | bytes 589828
  739.1 17.0 %copy-start.5 = (bf16[1,1536,768]{2,1,0:T(8,128)(2,1)S(1)}, bf16[1,1536,768]{2,1,0:T(8,128)(2,1)}, u32[]{:S(2)}) copy-start(bf16[1,1536,768]{2,1,0:T(8,128)(2,1)} %all-gather.19.cloned.1.call-done) | copy-start | bytes 7077892
  742.3 13.8 %copy-start.77 = (bf16[128,1536]{1,0:T(8,128)(2,1)S(1)}, bf16[128,1536]{1,0:T(8,128)(2,1)}, u32[]{:S(2)}) copy-start(bf16[128,1536]{1,0:T(8,128)(2,1)} %copy-done.76) | copy-start | bytes 1179652
  755.7 172.2 %all-reduce.49.cloned.1.call-start = ((), (), s32[]{:S(2)}) async-start(), calls=%async_computation.8 | async-start | bytes 2813952 | tf_op jit(solution)/shard_map/psum | solution.py:393
  761.3 77.7 %copy-start.121 = (bf16[768,768]{1,0:T(8,128)(2,1)S(1)}, bf16[768,768]{1,0:T(8,128)(2,1)}, u32[]{:S(2)}) copy-start(bf16[768,768]{1,0:T(8,128)(2,1)} %all-reduce.45.cloned.1.call-done) | copy-start | bytes 3538948
  (295 other events, 1014.3 us)
Sparse Core Ops, SparseCore 0:
  9.7 14.2 all-gather.12
  25.5 12.1 all-gather.16
  40.8 62.7 all-gather.14
  104.9 9.5 all-gather.18
  147.5 61.7 all-gather.20
  243.3 58.8 all-gather.24
  380.2 60.5 all-gather.22
  483.5 58.0 all-gather.26
  610.8 61.4 all-gather.28
  675.6 80.0 all-reduce.44
  759.6 79.3 all-reduce.46
  843.1 84.8 all-reduce.48

commit v2 on v1

--- a/solution.py
+++ b/solution.py
@@ -381,16 +381,15 @@
     left_norm, gate_all, two_all, left_out, grad_all = joined
     own_out = lax.psum(to_owner(col_product(left_out, grad_all)), "dp")
     gate_part = to_owner(col_product(left_norm, gate_all))
-    gate_part, own_out = lax.optimization_barrier((gate_part, own_out))
-    own_gate = lax.psum(gate_part, "dp")
     small_rows = left_norm.shape[1] // lax.axis_size("shard")
     rest_part = to_owner(
         jnp.concatenate(
             [col_product(left_norm, two_all), pack_small(small_total, small_rows)], axis=1
         )
     )
-    rest_part, own_gate = lax.optimization_barrier((rest_part, own_gate))
-    own_rest = lax.psum(rest_part, "dp").astype(jnp.float32)
+    gate_part, rest_part, own_out = lax.optimization_barrier((gate_part, rest_part, own_out))
+    own_gate, own_rest = lax.psum((gate_part, rest_part), "dp")
+    own_rest = own_rest.astype(jnp.float32)
     gains, taps, biases, steps, rates, skips, ggains = unpack_small(
         own_rest[:, XC + H :], small_total
     )

time: 963 us -> 976 us (1.013)
  waiting for transfers between devices: 334 us -> 352 us
    psum x1, waiting for transfers between devices: 13.4 us -> 75.5 us  [per_device(): own_out = lax.psum(to_owner(col_product(left_out, grad_all)), 'dp')]
    psum x2 -> x1, waiting for transfers between devices: 162 us -> 113 us  [per_device(): own_gate, own_rest = lax.psum((gate_part, rest_part), 'dp')]
    unnamed x645 -> x659, local copies, waits for them, and re-layouts: 27.4 us -> 26.5 us
  transfers between devices with their start and end apart: 25 -> 24, of which waited for: 12 -> 12; matrix products, arithmetic and copies ran while one was open for 38% -> 37% of each run, Pallas kernels for 0% -> 0%
where the time goes in v2:
time: 976 us; the launch traced here: 960 us
  waiting for transfers between devices  352 us (36%)
  other arithmetic  207 us (21%)
  local copies, waits for them, and re-layouts  192 us (20%)
  matrix products  142 us (15%)
  starting transfers between devices  29.9 us (3%)
  between operations  26.4 us (3%)
  blocking collectives  12.1 us (1%)
    all_gather x3, waiting for transfers between devices, entering(): everything = lax.all_gather(payload.astype(jnp.bfloat16), 'dp')  113 us
    psum x1, waiting for transfers between devices, per_device(): own_gate, own_rest = lax.psum((gate_part, rest_part), 'dp')  113 us
    psum x1, waiting for transfers between devices, per_device(): own_out = lax.psum(to_owner(col_product(left_out, grad_all)), 'dp')  75.5 us
    dot_general x12, matrix products, mix_out(): jnp.einsum('hij,jhp->ihp', weight * inner_cb[None], scaled, precision=high)  35.6 us
    all_gather x3, waiting for transfers between devices, carried_in(): lax.all_gather(grad_state.reshape(H * P_SIZE, N).astype(jnp.bfloat16), 'dp')  35.2 us
    ppermute x10, starting transfers between devices, passed_along(): lax.ppermute(value, axis, [(source, source + steps) for source in range(f...  28.2 us
    unnamed x659, local copies, waits for them, and re-layouts  26.5 us
    reduce_sum x6, other arithmetic, weighted(): jnp.sum(states.astype(jnp.float32) * factor[:, :, None, None], axis=0)  23.4 us
  transfers between devices with their start and end apart: 24, of which 12 were waited for; matrix products, arithmetic and copies ran while one was open for 37% of the time, Pallas kernels for 0%

profile of v2, /device:TPU:0, one launch (start us, length us, event | category | flops | bytes accessed | tf_op | source)
XLA Modules:
  0.0 960.3 jit_solution(13279749555320788203)
XLA Ops:
  21.2 3.0 all-reduce.41
  30.3 4.7 collective-permute-start
  56.1 47.4 %all-gather.15.cloned.1.call-done = bf16[8,1552,128]{2,1,0:T(8,128)(2,1)} async-done(((bf16[1,1552,128]{2,1,0:T(8,128)(2,1)}), bf16[8,1552,128]{2,1,0:T(8,128)(2,1)}) %all-gather.15.cloned.1.call-update) | async-done | bytes 3178512 | tf_op jit(solution)/shard_map/all_gather | solution.py:46
  105.2 3.9 multiply_reduce_fusion.2
  111.6 3.0 all-gather.19.cloned.1.call-done
  117.0 3.6 collective-permute-start.1
  122.6 2.7 collective-permute-done.1
  128.7 3.7 collective-permute-start.2
  158.8 3.8 fusion.103
  162.6 46.7 %all-gather.21.cloned.1.call-done = bf16[8,1552,128]{2,1,0:T(8,128)(2,1)} async-done(((bf16[1,1552,128]{2,1,0:T(8,128)(2,1)}), bf16[8,1552,128]{2,1,0:T(8,128)(2,1)}) %all-gather.21.cloned.1.call-update) | async-done | bytes 3178512 | tf_op jit(solution)/shard_map/all_gather | solution.py:46
  212.0 3.9 multiply_reduce_fusion.1
  222.5 4.4 fusion.142
  229.2 3.0 multiply_reduce_fusion.44
  234.2 2.7 multiply_reduce_fusion.23
  248.9 2.8 compare_convert_fusion.15
  251.7 2.7 compare_convert_fusion
  272.8 3.7 collective-permute-start.3
  276.6 3.1 fusion.210
  287.1 15.1 %all-gather.25.cloned.1.call-done = bf16[12288,128]{1,0:T(8,128)(2,1)} async-done(((bf16[1536,128]{1,0:T(8,128)(2,1)}), bf16[12288,128]{1,0:T(8,128)(2,1)}) %all-gather.25.cloned.1.call-update) | async-done | bytes 3145744 | tf_op jit(solution)/shard_map/all_gather | solution.py:55
  302.2 3.9 fusion.2
  319.8 4.0 multiply_reduce_fusion.41
  357.0 5.1 collective-permute-start.4
  381.5 2.7 compare_convert_fusion.5
  404.8 4.2 multiply_convert_fusion.2
  422.1 18.8 %all-gather.23.cloned.1.call-done = bf16[8,1552,128]{2,1,0:T(8,128)(2,1)} async-done(((bf16[1,1552,128]{2,1,0:T(8,128)(2,1)}), bf16[8,1552,128]{2,1,0:T(8,128)(2,1)}) %all-gather.23.cloned.1.call-update) | async-done | bytes 3178512 | tf_op jit(solution)/shard_map/all_gather | solution.py:46
  447.2 3.9 multiply_reduce_fusion
  454.9 2.6 fusion.148
  459.9 3.7 multiply_reduce_fusion.37
  471.6 5.3 multiply_reduce_fusion.30
  500.8 2.9 fusion.106
  513.3 4.4 fusion.212
  525.4 16.3 %all-gather.27.cloned.1.call-done = bf16[12288,128]{1,0:T(8,128)(2,1)} async-done(((bf16[1536,128]{1,0:T(8,128)(2,1)}), bf16[12288,128]{1,0:T(8,128)(2,1)}) %all-gather.27.cloned.1.call-update) | async-done | bytes 3145744 | tf_op jit(solution)/shard_map/all_gather | solution.py:55
  541.6 3.9 fusion.1
  559.3 4.0 multiply_reduce_fusion.34
  593.0 6.6 collective-permute-done.8
  601.7 2.7 multiply_reduce_fusion.21
  652.2 3.0 convolution_convert_fusion.2
  657.8 3.3 fusion.214
  668.5 3.8 all-gather.29.cloned.1.call-done
  672.3 3.9 fusion
  687.0 3.8 multiply_reduce_fusion.27
  729.7 3.2 convolution_convert_fusion
  733.6 2.7 fusion.98
  739.1 3.1 add_convert_fusion.2
  742.2 2.8 add_convert_fusion
  745.1 75.5 %all-reduce.45.cloned.1.call-done = bf16[768,768]{1,0:T(8,128)(2,1)} async-done(((bf16[768,768]{1,0:T(8,128)(2,1)}), bf16[768,768]{1,0:T(8,128)(2,1)}) %all-reduce.45.cloned.1.call-update) | async-done | bytes 1179664 | tf_op jit(solution)/shard_map/psum | solution.py:382
  827.2 112.9 %all-reduce.47.cloned.1.call-done = (bf16[384,1831]{0,1:T(8,128)(2,1)}, bf16[1,384,1536]{2,1,0:T(8,128)(2,1)}) async-done(((bf16[384,1831]{0,1:T(8,128)(2,1)}, bf16[1,384,1536]{2,1,0:T(8,128)(2,1)}), (bf16[384,1831]{0,1:T(8,128)(2,1)}, bf16[1,384,1536]{2,1,0:T(8,128)(2,1)})) %all-reduce.47.cloned.1.call-update) | async-done | bytes 2585872 | tf_op jit(solution)/shard_map/psum | solution.py:391
  945.9 3.4 copy.650
  (1084 shorter events, 453.4 us)
Async XLA Ops:
  7.2 11.9 %copy-start.320 = (bf16[1,12]{1,0:T(2,128)(2,1)S(1)}, bf16[1,12]{1,0:T(2,128)(2,1)}, u32[]{:S(2)}) copy-start(bf16[1,12]{1,0:T(2,128)(2,1)} %param.24) | copy-start | bytes 76
  7.3 12.1 %copy-start.321 = (bf16[1,12]{1,0:T(2,128)(2,1)S(1)}, bf16[1,12]{1,0:T(2,128)(2,1)}, u32[]{:S(2)}) copy-start(bf16[1,12]{1,0:T(2,128)(2,1)} %param.25) | copy-start | bytes 76
  7.3 12.3 %copy-start.322 = (bf16[1,12]{1,0:T(2,128)(2,1)S(1)}, bf16[1,12]{1,0:T(2,128)(2,1)}, u32[]{:S(2)}) copy-start(bf16[1,12]{1,0:T(2,128)(2,1)} %param.26) | copy-start | bytes 76
  7.3 16.9 %copy-start.226 = (bf16[1,384,24]{1,2,0:T(8,128)(2,1)S(1)}, bf16[1,384,24]{1,2,0:T(8,128)(2,1)}, u32[]{:S(2)}) copy-start(bf16[1,384,24]{1,2,0:T(8,128)(2,1)} %param.21) | copy-start | bytes 55300
  7.3 20.6 %all-gather.13.cloned.1.call-start = ((), (), s32[]{:S(2)}) async-start(), calls=%async_computation | async-start | bytes 4128768 | tf_op jit(solution)/shard_map/all_gather | solution.py:324
  8.0 42.2 %all-gather.17.cloned.1.call-start = ((), (), s32[]{:S(2)}) async-start(), calls=%async_computation.2 | async-start | bytes 3538944 | tf_op jit(solution)/shard_map/all_gather | solution.py:323
  8.8 94.8 %all-gather.15.cloned.1.call-start = ((), (), s32[]{:S(2)}) async-start(), calls=%async_computation.1 | async-start | bytes 3575808 | tf_op jit(solution)/shard_map/all_gather | solution.py:46
  9.0 21.2 %copy-start.288 = (f32[128]{0:T(128)}, f32[128]{0:T(128)S(1)}, u32[]{:S(2)}) copy-start(f32[128]{0:T(128)S(1)} %add_rsqrt_fusion.5) | copy-start | bytes 1540
  11.0 19.3 %copy-start.153 = (f32[768]{0:T(1024)}, f32[768]{0:T(1024)S(1)}, u32[]{:S(2)}) copy-start(f32[768]{0:T(1024)S(1)} %convert_reduce_fusion.5) | copy-start | bytes 9220
  14.7 21.9 %copy-start.135 = (f32[1792]{0:T(1024)}, f32[1792]{0:T(1024)S(1)}, u32[]{:S(2)}) copy-start(f32[1792]{0:T(1024)S(1)} %get-tuple-element.160) | copy-start | bytes 21508
  14.7 21.9 %copy-start.141 = (f32[1792]{0:T(1024)}, f32[1792]{0:T(1024)S(1)}, u32[]{:S(2)}) copy-start(f32[1792]{0:T(1024)S(1)} %get-tuple-element.161) | copy-start | bytes 21508
  14.7 21.9 %copy-start.147 = (f32[1792]{0:T(1024)}, f32[1792]{0:T(1024)S(1)}, u32[]{:S(2)}) copy-start(f32[1792]{0:T(1024)S(1)} %get-tuple-element.162) | copy-start | bytes 21508
  30.3 6.1 collective-permute-start
  40.7 73.9 %all-gather.19.cloned.1.call-start = ((), (), s32[]{:S(2)}) async-start(), calls=%async_computation.3 | async-start | bytes 3538944 | tf_op jit(solution)/shard_map/all_gather | solution.py:332
  41.2 168.1 %all-gather.21.cloned.1.call-start = ((), (), s32[]{:S(2)}) async-start(), calls=%async_computation.4 | async-start | bytes 3575808 | tf_op jit(solution)/shard_map/all_gather | solution.py:46
  41.8 62.6 %copy-start.286 = (pred[8]{0:T(512)(128)(4,1)}, pred[8]{0:T(512)(128)(4,1)S(1)}, u32[]{:S(2)}) copy-start(pred[8]{0:T(512)(128)(4,1)S(1)} %get-tuple-element.361) | copy-start | bytes 28
  46.4 57.9 %copy-start.252 = (pred[8,8]{1,0:T(8,128)(4,1)}, pred[8,8]{1,0:T(8,128)(4,1)S(1)}, u32[]{:S(2)}) copy-start(pred[8,8]{1,0:T(8,128)(4,1)S(1)} %fusion.479) | copy-start | bytes 196
  52.5 58.1 %copy-start.31 = (f32[128,1536]{1,0:T(8,128)}, f32[128,1536]{1,0:T(8,128)S(1)}, u32[]{:S(2)}) copy-start(f32[128,1536]{1,0:T(8,128)S(1)} %fusion.46) | copy-start | bytes 2359300
  114.6 11.5 %copy-start.280 = (f32[24]{0:T(128)S(1)}, f32[24]{0:T(128)}, u32[]{:S(2)}) copy-start(f32[24]{0:T(128)} %copy-done.279) | copy-start | bytes 292
  114.6 12.6 %copy-start = (bf16[1,768,1792]{2,1,0:T(8,128)(2,1)S(1)}, bf16[1,768,1792]{2,1,0:T(8,128)(2,1)}, u32[]{:S(2)}) copy-start(bf16[1,768,1792]{2,1,0:T(8,128)(2,1)} %all-gather.13.cloned.1.call-done) | copy-start | bytes 8257540
  117.0 8.2 collective-permute-start.1
  128.7 7.3 collective-permute-start.2
  140.0 18.0 %copy-start.48 = (bf16[128,1792]{1,0:T(8,128)(2,1)}, bf16[128,1792]{1,0:T(8,128)(2,1)S(1)}, u32[]{:S(2)}) copy-start(bf16[128,1792]{1,0:T(8,128)(2,1)S(1)} %get-tuple-element.217) | copy-start | bytes 1376260
  147.4 154.8 %all-gather.25.cloned.1.call-start = ((), (), s32[]{:S(2)}) async-start(), calls=%async_computation.7 | async-start | bytes 3538944 | tf_op jit(solution)/shard_map/all_gather | solution.py:55
  158.0 52.1 %copy-start.208 = (f32[8,1,24]{2,1,0:T(1,128)S(1)}, f32[8,1,24]{2,1,0:T(1,128)}, u32[]{:S(2)}) copy-start(f32[8,1,24]{2,1,0:T(1,128)} %copy-done.207) | copy-start | bytes 2308
  158.8 51.9 %copy-start.253 = (pred[8,8]{1,0:T(8,128)(4,1)S(1)}, pred[8,8]{1,0:T(8,128)(4,1)}, u32[]{:S(2)}) copy-start(pred[8,8]{1,0:T(8,128)(4,1)} %copy-done.252) | copy-start | bytes 196
  158.8 51.9 %copy-start.287 = (pred[8]{0:T(512)(128)(4,1)S(1)}, pred[8]{0:T(512)(128)(4,1)}, u32[]{:S(2)}) copy-start(pred[8]{0:T(512)(128)(4,1)} %copy-done.286) | copy-start | bytes 28
  243.2 197.7 %all-gather.23.cloned.1.call-start = ((), (), s32[]{:S(2)}) async-start(), calls=%async_computation.5 | async-start | bytes 3575808 | tf_op jit(solution)/shard_map/all_gather | solution.py:46
  272.8 76.7 %collective-permute-start.3 = (bf16[128,768]{1,0:T(8,128)(2,1)}, bf16[128,768]{1,0:T(8,128)(2,1)}, u32[]{:S(2)}, u32[]{:S(2)}) collective-permute-start(bf16[128,768]{1,0:T(8,128)(2,1)} %fusion.191), channel_id=1, source_target_pairs={{0,16},{1,17},{2,18},{3,19},{4,20},{5,21},{6,22},{7,23},{8,24},{9,... | collective-permute-start | bytes 589832 | tf_op jit(solution)/shard_map/ppermute | solution.py:21
  332.5 14.5 %collective-permute-start.5 = (f32[3,1792]{1,0:T(4,128)}, f32[3,1792]{1,0:T(4,128)}, u32[]{:S(2)}, u32[]{:S(2)}) collective-permute-start(f32[3,1792]{1,0:T(4,128)} %pad_add_fusion.5), channel_id=1, source_target_pairs={{1,0},{2,1},{3,2},{4,3},{5,4},{6,5},{7,6},{9,8},{10,9},{11,10},{12... | collective-permute-start | bytes 64520 | tf_op jit(solution)/shard_map/ppermute | solution.py:21
  357.0 9.6 collective-permute-start.4
  380.0 161.7 %all-gather.27.cloned.1.call-start = ((), (), s32[]{:S(2)}) async-start(), calls=%async_computation.8 | async-start | bytes 3538944 | tf_op jit(solution)/shard_map/all_gather | solution.py:55
  388.3 32.0 %collective-permute-start.6 = (bf16[128,768]{1,0:T(8,128)(2,1)}, bf16[128,768]{1,0:T(8,128)(2,1)}, u32[]{:S(2)}, u32[]{:S(2)}) collective-permute-start(bf16[128,768]{1,0:T(8,128)(2,1)} %fusion.342), channel_id=1, source_target_pairs={{16,0},{17,1},{18,2},{19,3},{20,4},{21,5},{22,6},{23,7},{24,8},{25... | collective-permute-start | bytes 589832 | tf_op jit(solution)/shard_map/ppermute | solution.py:21
  483.3 189.0 %all-gather.29.cloned.1.call-start = ((), (), s32[]{:S(2)}) async-start(), calls=%async_computation.9 | async-start | bytes 3538944 | tf_op jit(solution)/shard_map/all_gather | solution.py:55
  571.9 14.5 %collective-permute-start.7 = (f32[3,1792]{1,0:T(4,128)}, f32[3,1792]{1,0:T(4,128)}, u32[]{:S(2)}, u32[]{:S(2)}) collective-permute-start(f32[3,1792]{1,0:T(4,128)} %pad_add_fusion.4), channel_id=1, source_target_pairs={{1,0},{2,1},{3,2},{4,3},{5,4},{6,5},{7,6},{9,8},{10,9},{11,10},{12... | collective-permute-start | bytes 64520 | tf_op jit(solution)/shard_map/ppermute | solution.py:21
  591.7 7.9 collective-permute-start.8
  610.7 209.9 %all-reduce.45.cloned.1.call-start = ((), (), s32[]{:S(2)}) async-start(), calls=%async_computation.6 | async-start | bytes 2359296 | tf_op jit(solution)/shard_map/psum | solution.py:382
  647.5 88.9 %collective-permute-start.12 = (bf16[768,768]{1,0:T(8,128)(2,1)}, bf16[768,768]{1,0:T(8,128)(2,1)}, u32[]{:S(2)}, u32[]{:S(2)}) collective-permute-start(bf16[768,768]{1,0:T(8,128)(2,1)} %constant_dynamic-slice_fusion), channel_id=1, source_target_pairs={{0,8},{8,0},{1,9},{9,1},{2,10},{10,2},{3,11},{11,3},{4,12},{12,4},... | collective-permute-start | bytes 3538952 | tf_op jit(solution)/shard_map/ppermute | solution.py:68
  656.4 82.7 %collective-permute-start.10 = (bf16[384,1536]{1,0:T(8,128)(2,1)}, bf16[384,1536]{1,0:T(8,128)(2,1)}, u32[]{:S(2)}, u32[]{:S(2)}) collective-permute-start(bf16[384,1536]{1,0:T(8,128)(2,1)} %constant_dynamic-slice_fusion.1), channel_id=1, source_target_pairs={{0,8},{8,0},{1,9},{9,1},{2,10},{10,2},{3,11},{11,3},{4,12},{12,4},... | collective-permute-start | bytes 3538952 | tf_op jit(solution)/shard_map/ppermute | solution.py:68
  699.2 27.9 %copy-start.30 = (bf16[128,768]{1,0:T(8,128)(2,1)S(1)}, bf16[128,768]{1,0:T(8,128)(2,1)}, u32[]{:S(2)}) copy-start(bf16[128,768]{1,0:T(8,128)(2,1)} %copy-done.27) | copy-start | bytes 589828
  699.2 27.9 %copy-start.45 = (bf16[128,768]{1,0:T(8,128)(2,1)S(1)}, bf16[128,768]{1,0:T(8,128)(2,1)}, u32[]{:S(2)}) copy-start(bf16[128,768]{1,0:T(8,128)(2,1)} %copy-done.43) | copy-start | bytes 589828
  699.2 27.9 %copy-start.116 = (f32[128,768]{1,0:T(8,128)S(1)}, f32[128,768]{1,0:T(8,128)}, u32[]{:S(2)}) copy-start(f32[128,768]{1,0:T(8,128)} %fusion.36) | copy-start | bytes 1179652
  699.2 27.9 %copy-start.159 = (f32[768]{0:T(1024)S(1)}, f32[768]{0:T(1024)}, u32[]{:S(2)}) copy-start(f32[768]{0:T(1024)} %copy-done.153) | copy-start | bytes 9220
  702.8 24.4 %copy-start.294 = (f32[128]{0:T(128)S(1)}, f32[128]{0:T(128)}, u32[]{:S(2)}) copy-start(f32[128]{0:T(128)} %fusion.489) | copy-start | bytes 1540
  712.5 13.4 %collective-permute-start.9 = (f32[3,1792]{1,0:T(4,128)}, f32[3,1792]{1,0:T(4,128)}, u32[]{:S(2)}, u32[]{:S(2)}) collective-permute-start(f32[3,1792]{1,0:T(4,128)} %pad_add_fusion.3), channel_id=1, source_target_pairs={{1,0},{2,1},{3,2},{4,3},{5,4},{6,5},{7,6},{9,8},{10,9},{11,10},{12... | collective-permute-start | bytes 64520 | tf_op jit(solution)/shard_map/ppermute | solution.py:21
  736.4 5.8 collective-permute-start.11
  739.0 201.2 %all-reduce.47.cloned.1.call-start = ((), (), s32[]{:S(2)}) async-start(), calls=%async_computation.10 | async-start | bytes 5173248 | tf_op jit(solution)/shard_map/psum | solution.py:391
  745.1 75.6 %copy-start.127 = (bf16[128,768]{1,0:T(8,128)(2,1)S(1)}, bf16[128,768]{1,0:T(8,128)(2,1)}, u32[]{:S(2)}) copy-start(bf16[128,768]{1,0:T(8,128)(2,1)} %copy-done.126) | copy-start | bytes 589828
  (302 other events, 992.2 us)
Sparse Core Ops, SparseCore 0:
  9.7 14.2 all-gather.12
  25.5 12.1 all-gather.16
  40.8 62.7 all-gather.14
  105.0 9.5 all-gather.18
  147.5 61.7 all-gather.20
  243.3 58.8 all-gather.24
  380.1 60.7 all-gather.22
  483.4 58.1 all-gather.26
  610.9 61.4 all-gather.28
  739.1 81.4 all-reduce.44
  825.4 114.7 all-reduce.46
